TPU v7x, 128 devices: a whole 4x4x4 slice. The times are simulated.
128 devices in a mesh: fsdp: 2 (over core), ctx: 16 (over y, x), tp: 4 (over z).
Axes of the slice: x: 4, y: 4, z: 4, core: 2. Of those that a mesh axis runs over, the one named last changes fastest.
Arguments:
- tokens: bfloat16 [2, 2, 1024, 2048], P(None, 'fsdp', 'ctx'), may hold values from -6 to 6
- routes: int32 [2, 2, 1024, 8], P(None, 'fsdp', 'ctx'), may hold values from 0 to 15, all different within a row; in each aligned block of 64 rows (0 to 63, 64 to 127, ..., all dimensions but the last counted through in order) at most 48 rows name the same one
- cotangent: bfloat16 [2, 2, 1024, 2048], P(None, 'fsdp', 'ctx'), may hold values from -6 to 6
- qkv_weight: bfloat16 [3, 2048, 2048], P(None, 'fsdp', 'tp'), may hold values from -0.125 to 0.125
- out_weight: bfloat16 [2048, 2048], P('fsdp', 'tp'), may hold values from -3 to 3
- norm_gains: bfloat16 [2, 2048], P(None, 'fsdp'), may hold values from 0.5 to 1.5
- qk_gains: bfloat16 [2, 128], P(None, 'fsdp'), may hold values from 0.5 to 1.5
- router_weight: bfloat16 [16, 2048], P(None, 'fsdp'), may hold values from -0.0625 to 0.0625
- expert_in: bfloat16 [16, 2, 2048, 1024], P('ctx', None, 'fsdp', 'tp'), may hold values from -0.125 to 0.125
- expert_out: bfloat16 [16, 2048, 1024], P('ctx', 'fsdp', 'tp'), may hold values from -1.5 to 1.5
Outputs:
- layer_out: bfloat16 [2, 2, 1024, 2048], P(None, 'fsdp', 'ctx')
- grad_tokens: float32 [2, 2, 1024, 2048], P(None, 'fsdp', 'ctx')
- grad_qkv: float32 [3, 2048, 2048], P(None, 'fsdp', 'tp')
- grad_out_proj: float32 [2048, 2048], P('fsdp', 'tp')
- grad_norm_gains: float32 [2, 2048], P(None, 'fsdp')
- grad_qk_gains: float32 [2, 128], P(None, 'fsdp')
- grad_router: float32 [16, 2048], P(None, 'fsdp')
- grad_expert_in: float32 [16, 2, 2048, 1024], P('ctx', None, 'fsdp', 'tp')
- grad_expert_out: float32 [16, 2048, 1024], P('ctx', 'fsdp', 'tp')
Inputs may be any that keep to these rules, and one draw needn't show every extreme that they name: `routes`: each row names 8 different experts. In every aligned block of 64 positions of a sequence no expert is named by more than 48 rows, a bound that some block reaches.
All inputs are finite; a program needn't handle non-finite values.
Results may differ from a plain program's by a relative error of at most 0.025.
Values may be sent and summed in bfloat16 or wider, within the bound.
A program may use at most 256 MiB of HBM per device.

v0:
```python
from functools import partial
import math

import jax
import jax.numpy as jnp
from jax import lax
from jax.sharding import PartitionSpec as P

HEAD_DIM = 128
EXPERTS = 16
TOP = 8


EPS = 1e-06
BASE = 10000.0


def norm_apply(values, scale_gain):
    return values * lax.rsqrt(jnp.mean(values * values, axis=-1, keepdims=True) + EPS) * scale_gain


def rotate(values, positions):
    half_dim = values.shape[-1] // 2
    frequency = BASE ** (-(jnp.arange(half_dim, dtype=jnp.float32) * 2.0 / values.shape[-1]))
    rotation = positions.astype(jnp.float32)[:, None] * frequency[None, :]
    cosine = jnp.cos(rotation)[:, None, :]
    sine_part = jnp.sin(rotation)[:, None, :]
    first_half = values[..., :half_dim]
    second = values[..., half_dim:]
    return jnp.concatenate(
        [first_half * cosine - second * sine_part, second * cosine + first_half * sine_part],
        axis=-1,
    )


def head_prep(raw_heads, scale_gain, positions):
    return rotate(norm_apply(raw_heads, scale_gain), positions)


def slot_tables(route_block, expert_count, capacity):
    seq_count, assigned = route_block.shape
    onehot = (
        route_block[:, :, None] == jnp.arange(expert_count, dtype=jnp.int32)[None, None, :]
    ).astype(jnp.int32)
    earlier = jnp.cumsum(onehot, axis=1) - onehot
    slot_index = jnp.sum(earlier * onehot, axis=2)
    seq_grid = jnp.broadcast_to(
        jnp.arange(seq_count, dtype=jnp.int32)[:, None], (seq_count, assigned)
    )
    assign_ids = jnp.arange(assigned, dtype=jnp.int32)[None, :]
    slot_table = (
        jnp.zeros((expert_count, seq_count, capacity), jnp.int32)
        .at[route_block, seq_grid, slot_index]
        .set(assign_ids)
    )
    filled = (
        jnp.zeros((expert_count, seq_count, capacity), jnp.bool_)
        .at[route_block, seq_grid, slot_index]
        .set(True)
    )
    return (slot_index, seq_grid, slot_table, filled)


def to_slots(source, slot_table, filled, divisor):
    seq_col = jnp.arange(source.shape[0], dtype=jnp.int32)[None, :, None]
    picked_rows = source[seq_col, slot_table // divisor]
    return jnp.where(filled[..., None], picked_rows, jnp.zeros((), source.dtype))


def run_experts(received, weight_up, weight_down):
    gate_up = jnp.einsum(
        "xcnd,xkdf->xcnkf", received, weight_up, preferred_element_type=jnp.float32
    )
    gate_pre = gate_up[:, :, :, 0, :]
    activated = gate_pre * jax.nn.sigmoid(gate_pre)
    hidden = (activated * gate_up[:, :, :, 1, :]).astype(jnp.bfloat16)
    result = jnp.einsum("xcnf,xdf->xcnd", hidden, weight_down, preferred_element_type=jnp.float32)
    return (result, received, gate_up)


def expert_backward(kept_rows, kept_both, grad_in, weight_up, weight_down):
    gate_pre = kept_both[:, :, :, 0, :]
    up_pre = kept_both[:, :, :, 1, :]
    sigmoid_gate = jax.nn.sigmoid(gate_pre)
    activated = gate_pre * sigmoid_gate
    hidden = (activated * up_pre).astype(jnp.bfloat16)
    hidden_grad = jnp.einsum(
        "xcnd,xdf->xcnf", grad_in, weight_down, preferred_element_type=jnp.float32
    )
    gate_grad = hidden_grad * up_pre * sigmoid_gate * (1.0 + gate_pre * (1.0 - sigmoid_gate))
    up_grad = hidden_grad * activated
    both_grad = jnp.stack([gate_grad, up_grad], axis=3).astype(jnp.bfloat16)
    rows_grad = jnp.einsum(
        "xcnkf,xkdf->xcnd", both_grad, weight_up, preferred_element_type=jnp.float32
    )
    grad_up = jnp.einsum(
        "xcnd,xcnkf->xkdf", kept_rows, both_grad, preferred_element_type=jnp.float32
    )
    grad_down = jnp.einsum("xcnd,xcnf->xdf", grad_in, hidden, preferred_element_type=jnp.float32)
    return (rows_grad, grad_up, grad_down)


def local(
    tokens,
    routes,
    cotangent,
    qkv_weight,
    out_weight,
    norm_gains,
    qk_gains,
    router_weight,
    expert_in,
    expert_out,
):
    micro_count, seq_count, group_rows, model_width = tokens.shape
    tok_rows = seq_count * group_rows
    capacity = 3 * group_rows // 4
    heads_here = qkv_weight.shape[2] // HEAD_DIM
    score_scale = 1.0 / math.sqrt(HEAD_DIM)
    positions = lax.axis_index("ctx") * group_rows + jnp.arange(group_rows, dtype=jnp.int32)
    prep_heads = partial(head_prep, positions=positions)
    no_batch = ((), ())

    def gather_weights():
        gathered = (
            lax.all_gather(qkv_weight, "fsdp", axis=1, tiled=True),
            lax.all_gather(out_weight, "fsdp", axis=0, tiled=True),
            lax.all_gather(norm_gains, "fsdp", axis=1, tiled=True),
            lax.all_gather(qk_gains, "fsdp", axis=1, tiled=True),
            lax.all_gather(router_weight, "fsdp", axis=1, tiled=True),
            lax.all_gather(expert_in, "fsdp", axis=2, tiled=True),
            lax.all_gather(expert_out, "fsdp", axis=1, tiled=True),
        )
        return tuple(gathered)

    outputs = []
    input_grads = []
    running = None
    for micro_index in range(micro_count):
        weights_now = gather_weights()
        qkv_full, out_full, gains_full, qk_full, router_full, up_full, down_full = weights_now
        inputs = tokens[micro_index].reshape(tok_rows, model_width).astype(jnp.float32)
        gain_pair = gains_full.astype(jnp.float32)
        gain_heads = qk_full.astype(jnp.float32)
        normed_one = norm_apply(inputs, gain_pair[0]).astype(jnp.bfloat16)
        projected = jnp.einsum(
            "rd,kdh->krh", normed_one, qkv_full, preferred_element_type=jnp.float32
        )
        raw_heads = projected.reshape(3, seq_count, group_rows, heads_here, HEAD_DIM)
        queries = prep_heads(raw_heads[0], gain_heads[0]).astype(jnp.bfloat16)
        key_local = prep_heads(raw_heads[1], gain_heads[1]).astype(jnp.bfloat16)
        value_local = raw_heads[2].astype(jnp.bfloat16)
        all_keys, all_values = (
            lax.all_gather(key_local, "ctx", axis=1, tiled=True),
            lax.all_gather(value_local, "ctx", axis=1, tiled=True),
        )
        scores = (
            jnp.einsum("sqhd,skhd->shqk", queries, all_keys, preferred_element_type=jnp.float32)
            * score_scale
        )
        top_score = jnp.max(scores, axis=-1, keepdims=True)
        exponent = jnp.exp(scores - top_score)
        row_total = jnp.sum(exponent, axis=-1, keepdims=True)
        log_total = top_score + jnp.log(row_total)
        attn_probs = (exponent / row_total).astype(jnp.bfloat16)
        head_mixed = jnp.einsum(
            "shqk,skhd->sqhd", attn_probs, all_values, preferred_element_type=jnp.float32
        )
        head_mixed = head_mixed.astype(jnp.bfloat16).reshape(tok_rows, heads_here * HEAD_DIM)
        attn_part = lax.dot_general(
            head_mixed, out_full, (((1,), (1,)), no_batch), preferred_element_type=jnp.float32
        )
        attended = lax.psum(attn_part, "tp")
        hidden_one = inputs + attended
        normed_two = norm_apply(hidden_one, gain_pair[1]).astype(jnp.bfloat16)
        logits = lax.dot_general(
            normed_two, router_full, (((1,), (1,)), no_batch), preferred_element_type=jnp.float32
        )
        router_probs = jax.nn.softmax(logits, axis=-1)
        route_rows = routes[micro_index].reshape(tok_rows, TOP)
        picker = (
            route_rows[:, :, None] == jnp.arange(EXPERTS, dtype=jnp.int32)[None, None, :]
        ).astype(jnp.float32)
        gate_values = jnp.sum(picker * router_probs[:, None, :], axis=2)
        route_block = routes[micro_index].reshape(seq_count, group_rows * TOP)
        slot_index, seq_grid, slot_table, filled = slot_tables(route_block, EXPERTS, capacity)
        sent_rows = to_slots(
            normed_two.reshape(seq_count, group_rows, model_width), slot_table, filled, TOP
        )
        slot_out, kept_rows, kept_both = run_experts(
            lax.all_to_all(sent_rows, "ctx", split_axis=0, concat_axis=1, tiled=True),
            up_full,
            down_full,
        )
        slot_back = lax.all_to_all(slot_out, "ctx", split_axis=1, concat_axis=0, tiled=True)
        picked = slot_back[route_block, seq_grid, slot_index]
        picked = picked.reshape(tok_rows, TOP, model_width)
        mixture = lax.psum(
            jnp.sum(gate_values[:, :, None] * picked, axis=1).astype(jnp.bfloat16), "tp"
        ).astype(jnp.float32)
        outputs.append(
            (hidden_one + mixture).astype(jnp.bfloat16).reshape(seq_count, group_rows, model_width)
        )
        weights_back = gather_weights()
        qkv_back, out_back, gains_back, qk_back, router_back, up_back, down_back = weights_back
        gain_pair_back = gains_back.astype(jnp.float32)
        gain_heads_back = qk_back.astype(jnp.float32)
        grad_rows_out = cotangent[micro_index].reshape(tok_rows, model_width).astype(jnp.float32)
        gate_grad_part = jnp.sum(grad_rows_out[:, None, :] * picked, axis=2)
        slot_grad = (gate_values[:, :, None] * grad_rows_out[:, None, :]).astype(jnp.bfloat16)
        slot_grad = slot_grad.reshape(seq_count, group_rows * TOP, model_width)
        sent_grads = to_slots(slot_grad, slot_table, filled, 1)
        got_grads = lax.all_to_all(sent_grads, "ctx", split_axis=0, concat_axis=1, tiled=True)
        rows_grad, grad_up, grad_down = expert_backward(
            kept_rows, kept_both, got_grads, up_back, down_back
        )
        rows_back = lax.all_to_all(rows_grad, "ctx", split_axis=1, concat_axis=0, tiled=True)
        picked_grads = rows_back[route_block, seq_grid, slot_index]
        picked_grads = picked_grads.reshape(tok_rows, TOP, model_width)
        expert_side, gate_grad = lax.psum((jnp.sum(picked_grads, axis=1), gate_grad_part), "tp")
        prob_grad = jnp.sum(picker * gate_grad[:, :, None], axis=1)
        logit_grad = router_probs * (
            prob_grad - jnp.sum(router_probs * prob_grad, axis=-1, keepdims=True)
        )
        logit_grad = logit_grad.astype(jnp.bfloat16)
        grad_router = lax.dot_general(
            logit_grad, normed_two, (((0,), (0,)), no_batch), preferred_element_type=jnp.float32
        )
        normed_two_grad = expert_side + jnp.dot(
            logit_grad, router_back, preferred_element_type=jnp.float32
        )
        second_pull = jax.vjp(norm_apply, hidden_one, gain_pair_back[1])[1]
        hidden_norm_grad, gain_two_grad = second_pull(normed_two_grad)
        hidden_grad = grad_rows_out + hidden_norm_grad
        attended_grad = hidden_grad.astype(jnp.bfloat16)
        mixed_grad = jnp.dot(attended_grad, out_back, preferred_element_type=jnp.float32).astype(
            jnp.bfloat16
        )
        mixed_grad = mixed_grad.reshape(seq_count, group_rows, heads_here, HEAD_DIM)
        grad_out_proj = lax.dot_general(
            attended_grad, head_mixed, (((0,), (0,)), no_batch), preferred_element_type=jnp.float32
        )
        scores_again = (
            jnp.einsum("sqhd,skhd->shqk", queries, all_keys, preferred_element_type=jnp.float32)
            * score_scale
        )
        probs_again = jnp.exp(scores_again - log_total)
        value_grads_all = jnp.einsum(
            "shqk,sqhd->skhd",
            probs_again.astype(jnp.bfloat16),
            mixed_grad,
            preferred_element_type=jnp.float32,
        )
        prob_grads = jnp.einsum(
            "sqhd,skhd->shqk", mixed_grad, all_values, preferred_element_type=jnp.float32
        )
        inner_sum = jnp.sum(probs_again * prob_grads, axis=-1, keepdims=True)
        score_grads = (probs_again * (prob_grads - inner_sum)).astype(jnp.bfloat16)
        query_grads = (
            jnp.einsum("shqk,skhd->sqhd", score_grads, all_keys, preferred_element_type=jnp.float32)
            * score_scale
        )
        key_grads_all = (
            jnp.einsum("shqk,sqhd->skhd", score_grads, queries, preferred_element_type=jnp.float32)
            * score_scale
        )
        key_local_grad, value_local_grad = (
            lax.psum_scatter(
                key_grads_all.astype(jnp.bfloat16), "ctx", scatter_dimension=1, tiled=True
            ).astype(jnp.float32),
            lax.psum_scatter(
                value_grads_all.astype(jnp.bfloat16), "ctx", scatter_dimension=1, tiled=True
            ).astype(jnp.float32),
        )
        query_pull = jax.vjp(prep_heads, raw_heads[0], gain_heads_back[0])[1]
        raw_query_grad, gain_query_grad = query_pull(query_grads)
        key_pull = jax.vjp(prep_heads, raw_heads[1], gain_heads_back[1])[1]
        raw_key_grad, gain_key_grad = key_pull(key_local_grad)
        proj_grad = jnp.stack([raw_query_grad, raw_key_grad, value_local_grad])
        proj_grad = proj_grad.reshape(3, tok_rows, heads_here * HEAD_DIM).astype(jnp.bfloat16)
        grad_qkv = jnp.einsum(
            "rd,krh->kdh", normed_one, proj_grad, preferred_element_type=jnp.float32
        )
        normed_one_part = jnp.einsum(
            "krh,kdh->rd", proj_grad, qkv_back, preferred_element_type=jnp.float32
        )
        normed_one_grad, head_gain_grad = (
            lax.psum(normed_one_part.astype(jnp.bfloat16), "tp").astype(jnp.float32),
            lax.psum(jnp.stack([gain_query_grad, gain_key_grad]).astype(jnp.bfloat16), "tp").astype(
                jnp.float32
            ),
        )
        first_pull = jax.vjp(norm_apply, inputs, gain_pair_back[0])[1]
        input_norm_grad, gain_one_grad = first_pull(normed_one_grad)
        input_grads.append(
            (hidden_grad + input_norm_grad).reshape(seq_count, group_rows, model_width)
        )
        layer_grads = (
            grad_qkv,
            grad_out_proj,
            jnp.stack([gain_one_grad, gain_two_grad]),
            head_gain_grad,
            grad_router,
            grad_up,
            grad_down,
        )
        layer_grads = tuple(
            (
                lax.psum_scatter(
                    layer_grads[0].astype(jnp.bfloat16), "fsdp", scatter_dimension=1, tiled=True
                ).astype(jnp.float32),
                lax.psum_scatter(
                    layer_grads[1].astype(jnp.bfloat16), "fsdp", scatter_dimension=0, tiled=True
                ).astype(jnp.float32),
                lax.psum_scatter(
                    layer_grads[2].astype(jnp.bfloat16), "fsdp", scatter_dimension=1, tiled=True
                ).astype(jnp.float32),
                lax.psum_scatter(
                    layer_grads[3].astype(jnp.bfloat16), "fsdp", scatter_dimension=1, tiled=True
                ).astype(jnp.float32),
                lax.psum_scatter(
                    layer_grads[4].astype(jnp.bfloat16), "fsdp", scatter_dimension=1, tiled=True
                ).astype(jnp.float32),
                lax.psum_scatter(
                    layer_grads[5].astype(jnp.bfloat16), "fsdp", scatter_dimension=2, tiled=True
                ).astype(jnp.float32),
                lax.psum_scatter(
                    layer_grads[6].astype(jnp.bfloat16), "fsdp", scatter_dimension=1, tiled=True
                ).astype(jnp.float32),
            )
        )
        if running is None:
            running = layer_grads
        else:
            running = tuple((earlier + latest for earlier, latest in zip(running, layer_grads)))
    summed = (
        lax.psum(running[0].astype(jnp.bfloat16), "ctx").astype(jnp.float32),
        lax.psum(running[1].astype(jnp.bfloat16), "ctx").astype(jnp.float32),
        lax.psum(running[2].astype(jnp.bfloat16), "ctx").astype(jnp.float32),
        lax.psum(running[3].astype(jnp.bfloat16), "ctx").astype(jnp.float32),
        lax.psum(running[4].astype(jnp.bfloat16), "ctx").astype(jnp.float32),
    )
    finals = tuple(summed) + (running[5], running[6])
    return (jnp.stack(outputs), jnp.stack(input_grads)) + tuple(finals)


def solution(mesh):
    in_specs = (
        P(None, "fsdp", "ctx", None),
        P(None, "fsdp", "ctx", None),
        P(None, "fsdp", "ctx", None),
        P(None, "fsdp", "tp"),
        P("fsdp", "tp"),
        P(None, "fsdp"),
        P(None, "fsdp"),
        P(None, "fsdp"),
        P("ctx", None, "fsdp", "tp"),
        P("ctx", "fsdp", "tp"),
    )
    out_specs = (
        P(None, "fsdp", "ctx", None),
        P(None, "fsdp", "ctx", None),
        P(None, "fsdp", "tp"),
        P("fsdp", "tp"),
        P(None, "fsdp"),
        P(None, "fsdp"),
        P(None, "fsdp"),
        P("ctx", None, "fsdp", "tp"),
        P("ctx", "fsdp", "tp"),
    )
    return jax.shard_map(local, mesh=mesh, in_specs=in_specs, out_specs=out_specs, check_vma=False)
```

profile of v0, /device:TPU:1, one launch (start us, length us, event | category | flops | bytes accessed | tf_op | source)
XLA Modules:
  0.0 1642.0 jit_solution(11827716652427747041)
XLA Ops:
  13.3 19.5 %all-gather.10.cloned.1.call-done = bf16[3,2048,512]{2,1,0:T(8,128)(2,1)} async-done(((bf16[3,1024,512]{2,1,0:T(8,128)(2,1)}), bf16[3,2048,512]{2,1,0:T(8,128)(2,1)}) %all-gather.10.cloned.1.call-update) | async-done | bytes 6291472 | tf_op jit(solution)/shard_map/all_gather | solution.py:126
  51.8 25.3 %scatter_fusion.3 = s32[16,48]{1,0:T(8,128)S(1)} fusion(s32[16,48]{1,0:T(8,128)S(1)} %broadcast.1058.clone, s32[512]{0:T(512)S(1)} %bitcast.697, s32[512]{0:T(512)S(1)} %iota.38), kind=kCustom, calls=%fused_computation.11 | custom fusion | bytes 10240 | tf_op jit(solution)/shard_map/scatter | solution.py:54
  89.2 42.4 %all-gather.22.cloned.1.call-done = bf16[1,1024,4,128]{3,1,2,0:T(8,128)(2,1)} async-done(((bf16[1,64,4,128]{3,1,2,0:T(8,128)(2,1)}), bf16[1,1024,4,128]{3,1,2,0:T(8,128)(2,1)}) %all-gather.22.cloned.1.call-update) | async-done | bytes 1048592 | tf_op jit(solution)/shard_map/all_gather | solution.py:155
  133.3 42.8 %all-gather.14.cloned.1.call-done = bf16[1,1024,4,128]{3,1,2,0:T(8,128)(2,1)} async-done(((bf16[1,64,4,128]{3,1,2,0:T(8,128)(2,1)}), bf16[1,1024,4,128]{3,1,2,0:T(8,128)(2,1)}) %all-gather.14.cloned.1.call-update) | async-done | bytes 1048592 | tf_op jit(solution)/shard_map/all_gather | solution.py:154
  178.2 42.3 %all-gather.12.cloned.1.call-done = bf16[1,1024,4,128]{3,1,2,0:T(8,128)(2,1)} async-done(((bf16[1,64,4,128]{3,1,2,0:T(8,128)(2,1)}), bf16[1,1024,4,128]{3,1,2,0:T(8,128)(2,1)}) %all-gather.12.cloned.1.call-update) | async-done | bytes 1048592 | tf_op jit(solution)/shard_map/all_gather | solution.py:155
  241.5 25.9 %scatter_fusion.2 = pred[16,48]{1,0:T(8,128)(4,1)S(1)} fusion(pred[16,48]{1,0:T(8,128)(4,1)S(1)} %broadcast.1053.clone, s32[512]{0:T(512)S(1)} %bitcast.698, pred[512]{0:T(512)(128)(4,1)S(1)} %broadcast.1055), kind=kCustom, calls=%fused_computation.10 | custom fusion | bytes 5632 | tf_op jit(solution)/shard_map/scatter | solution.py:59
  270.6 16.4 all-reduce.30.cloned.1.call-done
  330.2 25.9 %scatter_fusion = pred[16,48]{1,0:T(8,128)(4,1)S(1)} fusion(pred[16,48]{1,0:T(8,128)(4,1)S(1)} %broadcast.1053.clone.1, s32[512]{0:T(512)S(1)} %bitcast.699, pred[512]{0:T(512)(128)(4,1)S(1)} %broadcast.1055), kind=kCustom, calls=%fused_computation.8 | custom fusion | bytes 5632 | tf_op jit(solution)/shard_map/scatter | solution.py:59
  356.1 25.3 %scatter_fusion.1 = s32[16,48]{1,0:T(8,128)S(1)} fusion(s32[16,48]{1,0:T(8,128)S(1)} %broadcast.1058.clone.1, s32[512]{0:T(512)S(1)} %bitcast.700, s32[512]{0:T(512)S(1)} %iota.37), kind=kCustom, calls=%fused_computation.9 | custom fusion | bytes 10240 | tf_op jit(solution)/shard_map/scatter | solution.py:54
  416.4 43.5 %all_to_all.84 = bf16[16,1,48,2048]{3,2,1,0:T(8,128)(2,1)} all-to-all(bf16[16,1,48,2048]{3,2,1,0:T(8,128)(2,1)} %get-tuple-element.183), channel_id=1, replica_groups=mesh['fsdp'=2,'ctx'=16,'tp'=4] {'ctx'}, dimensions={0} | all-to-all | bytes 6291456 | tf_op jit(solution)/shard_map/all_to_all | solution.py:213
  465.1 35.8 %all-to-all-done = bf16[16,1,48,2048]{3,2,1,0:T(8,128)(2,1)} async-done(((bf16[16,1,48,2048]{3,2,1,0:T(8,128)(2,1)}), bf16[16,1,48,2048]{3,2,1,0:T(8,128)(2,1)}, u32[]{:S(2)}, u32[]{:S(2)}) %all-to-all-start) | async-done | bytes 3145760 | tf_op jit(solution)/shard_map/all_to_all | solution.py:191
  571.1 75.7 %all-to-all-done.5 = f32[1,16,48,2048]{3,2,0,1:T(8,128)} async-done(((f32[1,16,48,2048]{3,2,0,1:T(8,128)}), f32[1,16,48,2048]{3,2,0,1:T(8,128)}, u32[]{:S(2)}, u32[]{:S(2)}) %all-to-all-start.5) | async-done | bytes 6291488 | tf_op jit(solution)/shard_map/all_to_all | solution.py:217
  657.4 79.8 %all-to-all-done.7 = f32[1,16,48,2048]{3,2,0,1:T(8,128)} async-done(((f32[1,16,48,2048]{3,2,0,1:T(8,128)}), f32[1,16,48,2048]{3,2,0,1:T(8,128)}, u32[]{:S(2)}, u32[]{:S(2)}) %all-to-all-start.7) | async-done | bytes 6291488 | tf_op jit(solution)/shard_map/all_to_all | solution.py:217
  747.6 74.9 %all-to-all-done.1 = f32[1,16,48,2048]{3,2,0,1:T(8,128)} async-done(((f32[1,16,48,2048]{3,2,0,1:T(8,128)}), f32[1,16,48,2048]{3,2,0,1:T(8,128)}, u32[]{:S(2)}, u32[]{:S(2)}) %all-to-all-start.1) | async-done | bytes 6291488 | tf_op jit(solution)/shard_map/all_to_all | solution.py:195
  871.2 45.6 %all-to-all-done.3 = f32[1,16,48,2048]{3,2,0,1:T(8,128)} async-done(((f32[1,16,48,2048]{3,2,0,1:T(8,128)}), f32[1,16,48,2048]{3,2,0,1:T(8,128)}, u32[]{:S(2)}, u32[]{:S(2)}) %all-to-all-start.3) | async-done | bytes 6291488 | tf_op jit(solution)/shard_map/all_to_all | solution.py:195
  948.1 28.7 %all-reduce.28.cloned.1.call-done = (f32[64,2048]{1,0:T(8,128)}, f32[64,2048]{1,0:T(8,128)}) async-done(((f32[64,2048]{1,0:T(8,128)}, f32[64,2048]{1,0:T(8,128)}), (f32[64,2048]{1,0:T(8,128)}, f32[64,2048]{1,0:T(8,128)})) %all-reduce.28.cloned.1.call-update) | async-done | bytes 1048592 | tf_op jit(solution)/shard_map/psum | solution.py:220
  1004.1 80.2 %all-reduce.34.cloned.1.call-done = (bf16[1,1024,4,128]{3,2,0,1:T(4,128)(2,1)}, bf16[1,1024,4,128]{3,2,0,1:T(4,128)(2,1)}) async-done(((bf16[1,1024,4,128]{3,2,0,1:T(4,128)(2,1)}, bf16[1,1024,4,128]{3,2,0,1:T(4,128)(2,1)}), (bf16[1,1024,4,128]{3,2,0,1:T(4,128)(2,1)}, bf16[1,1024,4,128]{3,2,0,1:T(4,128)(2,1)})) %all-reduce.34.cloned.1.call-update) | async-done | bytes 2097168
  1086.1 74.0 %reduce-scatter.25.cloned.1.call-done = bf16[1,64,4,128]{3,1,2,0:T(8,128)(2,1)} async-done(((bf16[1,1024,4,128]{3,1,2,0:T(8,128)(2,1)}), bf16[1,64,4,128]{3,1,2,0:T(8,128)(2,1)}) %reduce-scatter.25.cloned.1.call-update) | async-done | bytes 65552 | tf_op jit(solution)/shard_map/reduce_scatter | solution.py:268
  1161.0 75.1 %reduce-scatter.27.cloned.1.call-done = bf16[1,64,4,128]{3,1,2,0:T(8,128)(2,1)} async-done(((bf16[1,1024,4,128]{3,1,2,0:T(8,128)(2,1)}), bf16[1,64,4,128]{3,1,2,0:T(8,128)(2,1)}) %reduce-scatter.27.cloned.1.call-update) | async-done | bytes 65552 | tf_op jit(solution)/shard_map/reduce_scatter | solution.py:268
  1313.6 16.6 %reduce-scatter.33.cloned.1.call-done = bf16[1024,512]{1,0:T(8,128)(2,1)} async-done(((bf16[2048,512]{1,0:T(8,128)(2,1)}), bf16[1024,512]{1,0:T(8,128)(2,1)}) %reduce-scatter.33.cloned.1.call-update) | async-done | bytes 1048592 | tf_op jit(solution)/shard_map/reduce_scatter | solution.py:312
  1332.9 18.5 %reduce-scatter.31.cloned.1.call-done = bf16[3,1024,512]{1,2,0:T(8,128)(2,1)} async-done(((bf16[3,2048,512]{1,2,0:T(8,128)(2,1)}), bf16[3,1024,512]{1,2,0:T(8,128)(2,1)}) %reduce-scatter.31.cloned.1.call-update) | async-done | bytes 3145744 | tf_op jit(solution)/shard_map/reduce_scatter | solution.py:309
  1351.5 20.9 %reduce-scatter.29.cloned.1.call-done = bf16[3,1024,512]{1,2,0:T(8,128)(2,1)} async-done(((bf16[3,2048,512]{1,2,0:T(8,128)(2,1)}), bf16[3,1024,512]{1,2,0:T(8,128)(2,1)}) %reduce-scatter.29.cloned.1.call-update) | async-done | bytes 3145744 | tf_op jit(solution)/shard_map/reduce_scatter | solution.py:309
  1521.0 61.2 %all-reduce.17 = (bf16[2,1024]{1,0:T(2,128)(2,1)S(1)}, bf16[2,64]{1,0:T(2,128)(2,1)S(1)}, bf16[16,1024]{1,0:T(8,128)(2,1)S(1)}) all-reduce(bf16[2,1024]{1,0:T(2,128)(2,1)S(1)} %add_convert_fusion.9, bf16[2,64]{1,0:T(2,128)(2,1)S(1)} %add_convert_fusion.10, ...), channel_id=1, replica_groups=mesh['fsdp'=2,'ctx'=16,'tp'=4] {'ctx'}, use_global_device_ids=true, to_apply=%region_74.75 | all-reduce | flops 18560 | bytes 74240 | tf_op jit(solution)/shard_map/psum | solution.py:339
  1584.0 44.4 %all-reduce.32.cloned.1.call-done = (bf16[3,1024,512]{1,2,0:T(8,128)(2,1)}, bf16[1024,512]{1,0:T(8,128)(2,1)}) async-done(((bf16[3,1024,512]{1,2,0:T(8,128)(2,1)}, bf16[1024,512]{1,0:T(8,128)(2,1)}), (bf16[3,1024,512]{1,2,0:T(8,128)(2,1)}, bf16[1024,512]{1,0:T(8,128)(2,1)})) %all-reduce.32.cloned.1.call-update) | async-done | bytes 4194320 | tf_op jit(solution)/shard_map/psum | solution.py:337
  (550 shorter events, 583.9 us)
Async XLA Ops:
  45.5 130.5 %all-gather.14.cloned.1.call-start = ((), (), s32[]{:S(2)}) async-start(), calls=%async_computation.26 | async-start | bytes 1114112 | tf_op jit(solution)/shard_map/all_gather | solution.py:154
  46.3 174.2 %all-gather.12.cloned.1.call-start = ((), (), s32[]{:S(2)}) async-start(), calls=%async_computation.25 | async-start | bytes 1114112 | tf_op jit(solution)/shard_map/all_gather | solution.py:155
  47.0 189.4 %all-gather.16.cloned.1.call-start = ((), (), s32[]{:S(2)}) async-start(), calls=%async_computation.27 | async-start | bytes 3145728 | tf_op jit(solution)/shard_map/all_gather | solution.py:127
  47.6 239.4 %all-reduce.30.cloned.1.call-start = ((), (), s32[]{:S(2)}) async-start(), calls=%async_computation.49 | async-start | bytes 2097152 | tf_op jit(solution)/shard_map/psum | solution.py:173
  553.3 93.5 %all-to-all-start.5 = ((f32[1,16,48,2048]{3,2,0,1:T(8,128)}), f32[1,16,48,2048]{3,2,0,1:T(8,128)}, u32[]{:S(2)}, u32[]{:S(2)}) async-start(f32[1,16,48,2048]{3,2,0,1:T(8,128)} %convolution_bitcast_fusion.3), calls=%async_computation.5 | async-start | bytes 12582912 | tf_op jit(solution)/shard_map/all_to_all | solution.py:217
  822.5 94.4 %all-to-all-start.3 = ((f32[1,16,48,2048]{3,2,0,1:T(8,128)}), f32[1,16,48,2048]{3,2,0,1:T(8,128)}, u32[]{:S(2)}, u32[]{:S(2)}) async-start(f32[1,16,48,2048]{3,2,0,1:T(8,128)} %convolution_bitcast_fusion), calls=%async_computation.3 | async-start | bytes 12582912 | tf_op jit(solution)/shard_map/all_to_all | solution.py:195
  830.1 146.7 %all-reduce.28.cloned.1.call-start = ((), (), s32[]{:S(2)}) async-start(), calls=%async_computation.48 | async-start | bytes 2097152 | tf_op jit(solution)/shard_map/psum | solution.py:220
  927.1 157.2 %all-reduce.34.cloned.1.call-start = ((), (), s32[]{:S(2)}) async-start(), calls=%async_computation.51 | async-start | bytes 4194304
  992.8 167.3 %reduce-scatter.25.cloned.1.call-start = ((), (), s32[]{:S(2)}) async-start(), calls=%async_computation.32 | async-start | bytes 1114112 | tf_op jit(solution)/shard_map/reduce_scatter | solution.py:268
  996.6 239.4 %reduce-scatter.27.cloned.1.call-start = ((), (), s32[]{:S(2)}) async-start(), calls=%async_computation.33 | async-start | bytes 1114112 | tf_op jit(solution)/shard_map/reduce_scatter | solution.py:268
  1000.5 295.5 %all-reduce.36.cloned.1.call-start = ((), (), s32[]{:S(2)}) async-start(), calls=%async_computation.52 | async-start | bytes 2097152 | tf_op jit(solution)/shard_map/psum | solution.py:198
  1254.1 97.4 %reduce-scatter.31.cloned.1.call-start = ((), (), s32[]{:S(2)}) async-start(), calls=%async_computation.35 | async-start | bytes 9437184 | tf_op jit(solution)/shard_map/reduce_scatter | solution.py:309
  1258.7 113.6 %reduce-scatter.29.cloned.1.call-start = ((), (), s32[]{:S(2)}) async-start(), calls=%async_computation.34 | async-start | bytes 9437184 | tf_op jit(solution)/shard_map/reduce_scatter | solution.py:309
  1263.9 124.1 %reduce-scatter.47.cloned.1.call-start = ((), (), s32[]{:S(2)}) async-start(), calls=%async_computation.43 | async-start | bytes 1572864 | tf_op jit(solution)/shard_map/reduce_scatter | solution.py:327
  1268.8 134.7 %reduce-scatter.45.cloned.1.call-start = ((), (), s32[]{:S(2)}) async-start(), calls=%async_computation.42 | async-start | bytes 1572864 | tf_op jit(solution)/shard_map/reduce_scatter | solution.py:327
  1272.9 146.7 %reduce-scatter.43.cloned.1.call-start = ((), (), s32[]{:S(2)}) async-start(), calls=%async_computation.41 | async-start | bytes 3145728 | tf_op jit(solution)/shard_map/reduce_scatter | solution.py:324
  1278.4 157.3 %reduce-scatter.41.cloned.1.call-start = ((), (), s32[]{:S(2)}) async-start(), calls=%async_computation.40 | async-start | bytes 3145728 | tf_op jit(solution)/shard_map/reduce_scatter | solution.py:324
  1283.6 166.5 %reduce-scatter.39.cloned.1.call-start = ((), (), s32[]{:S(2)}) async-start(), calls=%async_computation.39 | async-start | bytes 98304 | tf_op jit(solution)/shard_map/reduce_scatter | solution.py:321
  1284.5 179.3 %reduce-scatter.37.cloned.1.call-start = ((), (), s32[]{:S(2)}) async-start(), calls=%async_computation.38 | async-start | bytes 98304 | tf_op jit(solution)/shard_map/reduce_scatter | solution.py:321
  1285.3 192.2 %reduce-scatter.53.cloned.1.call-start = ((), (), s32[]{:S(2)}) async-start(), calls=%async_computation.46 | async-start | bytes 49152
  1286.2 205.0 %reduce-scatter.55.cloned.1.call-start = ((), (), s32[]{:S(2)}) async-start(), calls=%async_computation.47 | async-start | bytes 49152
  1287.0 218.4 %reduce-scatter.49.cloned.1.call-start = ((), (), s32[]{:S(2)}) async-start(), calls=%async_computation.44 | async-start | bytes 786432
  1298.7 221.3 %reduce-scatter.51.cloned.1.call-start = ((), (), s32[]{:S(2)}) async-start(), calls=%async_computation.45 | async-start | bytes 786432
  1299.8 328.6 %all-reduce.32.cloned.1.call-start = ((), (), s32[]{:S(2)}) async-start(), calls=%async_computation.50 | async-start | bytes 8388608 | tf_op jit(solution)/shard_map/psum | solution.py:337
  (121 other events, 6373.4 us)
Sparse Core Ops, SparseCore 0:
  9.7 23.0 all-gather.9
  44.9 42.0 all-gather.23
  89.7 41.8 all-gather.21
  134.2 41.8 all-gather.13
  178.6 41.8 all-gather.11
  222.0 14.4 all-gather.15
  241.4 45.5 all-reduce.29
  466.9 18.5 all-gather.17
  513.1 16.1 all-gather.19
  927.2 49.5 all-reduce.27
  992.9 91.3 all-reduce.33
  1088.3 71.8 reduce-scatter.24
  1163.9 72.0 reduce-scatter.26
  1249.9 46.0 all-reduce.35
  1298.7 14.7 reduce-scatter.34
  1316.5 13.6 reduce-scatter.32
  1333.0 18.4 reduce-scatter.30
  1353.8 18.4 reduce-scatter.28
  1375.3 12.6 reduce-scatter.46
  1390.9 12.5 reduce-scatter.44
  1405.9 13.6 reduce-scatter.42
  1422.0 13.6 reduce-scatter.40
  1493.4 11.9 reduce-scatter.48
  1523.9 104.4 all-reduce.31
  (5 shorter events, 57.5 us)
where the time goes:
time: 1650 us; the launch traced here: 1640 us
  waiting for transfers between devices  1030 us (62%)
  local copies, waits for them, and re-layouts  229 us (14%)
  blocking collectives  136 us (8%)
  matrix products  113 us (7%)
  other arithmetic  71.2 us (4%)
  starting transfers between devices  45.7 us (3%)
  between operations  17.5 us (1%)
    all_to_all x2, waiting for transfers between devices, local(): lax.all_to_all(rows_grad, 'ctx', split_axis=1, concat_axis=0, tiled=True)  155 us
    reduce_scatter x2, waiting for transfers between devices, local(): lax.psum_scatter(key_grads_all.astype(jnp.bfloat16), 'ctx', scatter_dimen...  149 us
    unnamed x34, waiting for transfers between devices  124 us
    all_to_all x2, waiting for transfers between devices, local(): lax.all_to_all(slot_out, 'ctx', split_axis=1, concat_axis=0, tiled=True)  121 us
    all_gather x2, waiting for transfers between devices, local(): lax.all_gather(value_local, 'ctx', axis=1, tiled=True)  84.7 us
    psum x1, blocking collectives, local(): lax.psum(running[2].astype(jnp.bfloat16), 'ctx').astype(jnp.float32)  61.2 us
    gather x4, local copies, waits for them, and re-layouts, to_slots(): picked_rows = source[seq_col, slot_table // divisor]  56.3 us
    all_gather x2, waiting for transfers between devices, local(): lax.all_gather(key_local, 'ctx', axis=1, tiled=True)  52.6 us
  transfers between devices with their start and end apart: 36, of which 34 were waited for; matrix products, arithmetic and copies ran while one was open for 19% of the time, Pallas kernels for 0%

commit v1 on v0

v1 whole, which is shorter than its diff:
```python
import math

import jax
import jax.numpy as jnp
import numpy as np
from jax import lax
from jax.experimental import pallas as pl
from jax.experimental.pallas import tpu as pltpu
from jax.sharding import PartitionSpec as P

EPS = 1e-06
BASE = 10000.0
HD = 128
E = 16
F32 = jnp.float32
BF = jnp.bfloat16


def rot(x, cos, sin):
    h = x.shape[-1] // 2
    a, b = x[..., :h], x[..., h:]
    return jnp.concatenate([a * cos - b * sin, b * cos + a * sin], axis=-1)


def rot_back(x, cos, sin):
    h = x.shape[-1] // 2
    a, b = x[..., :h], x[..., h:]
    return jnp.concatenate([a * cos + b * sin, b * cos - a * sin], axis=-1)


def inv_rms(v):
    return lax.rsqrt(jnp.mean(v * v, axis=-1, keepdims=True) + EPS)


def norm_back(v, g, du):
    r = inv_rms(v)
    gdu = g * du
    dv = r * gdu - r * r * r * v * jnp.mean(v * gdu, axis=-1, keepdims=True)
    return dv, du * v * r


def nt(a, b):
    return lax.dot_general(a, b, (((1,), (1,)), ((), ())), preferred_element_type=F32)


def tn(a, b):
    return lax.dot_general(a, b, (((0,), (0,)), ((), ())), preferred_element_type=F32)


def nn(a, b):
    return jnp.dot(a, b, preferred_element_type=F32)


def permute(x):
    w = x.shape[-1]
    return x.reshape(2, 4, 16, w).transpose(1, 0, 2, 3).reshape(128, w)


def unpermute(x):
    w = x.shape[-1]
    return x.reshape(4, 2, 16, w).transpose(1, 0, 2, 3).reshape(2, 64, w)


def to_pairs(x):
    return x.reshape(4, 2, 16, 4, HD).transpose(1, 3, 0, 2, 4).reshape(8, 64, HD)


def from_pairs(x):
    return x.reshape(2, 4, 4, 16, HD).transpose(2, 0, 3, 1, 4).reshape(128, 512)


def rope_tables():
    ctx = lax.axis_index("ctx")
    w = BASE ** (-(jnp.arange(64, dtype=F32) * 2.0 / HD))
    pos = (ctx * 64 + jnp.arange(64)).astype(F32)
    ang = pos[:, None] * w[None, :]
    tab = jnp.concatenate([jnp.cos(ang), jnp.sin(ang)], axis=1)
    tab = jnp.broadcast_to(tab.reshape(4, 1, 16, 128), (4, 2, 16, 128)).reshape(128, 128)
    return tab[:, None, :64], tab[:, None, 64:]


def chosen_mask(routes):
    t = lax.axis_index("tp")
    r = lax.dynamic_index_in_dim(routes.reshape(2, 4, 16, 8), t, 1, keepdims=False).reshape(32, 8)
    return jnp.any(r[:, :, None] == jnp.arange(E)[None, None, :], axis=1)


def quarter(x):
    t = lax.axis_index("tp")
    w = x.shape[-1]
    return lax.dynamic_index_in_dim(x.reshape(2, 4, 16, w), t, 1, keepdims=False).reshape(32, w)


MESH = pl.DeviceIdType.MESH
VM = pl.BlockSpec(memory_space=pltpu.VMEM)
ANY = pl.BlockSpec(memory_space=pl.ANY)
SCALE = 1.0 / math.sqrt(HD)


def place():
    f, c, t = lax.axis_index("fsdp"), lax.axis_index("ctx"), lax.axis_index("tp")
    return f, c, t, c // 4, c % 4


def own_pair():
    f, c, _, _, _ = place()
    return c // 8 == f


def hello():
    f, c, t, _, _ = place()
    bar = pltpu.get_barrier_semaphore()
    for k in range(1, 16):
        pl.semaphore_signal(bar, inc=1, device_id={"ctx": (c + k) % 16}, device_id_type=MESH)
    for k in range(1, 4):
        pl.semaphore_signal(bar, inc=1, device_id={"tp": (t + k) % 4}, device_id_type=MESH)
    for k in range(4):
        pl.semaphore_signal(bar, inc=1, device_id={"fsdp": 1 - f, "tp": (t + k) % 4}, device_id_type=MESH)

    @pl.when(c // 8 != f)
    def _():
        for j in range(8):
            pl.semaphore_signal(bar, inc=1, device_id={"fsdp": c // 8, "ctx": 8 * f + j}, device_id_type=MESH)


def greeted():
    f, c, _, _, _ = place()
    pl.semaphore_wait(pltpu.get_barrier_semaphore(), 22 + 8 * (c // 8 + f - 2 * (c // 8) * f))


class Heads:
    def __init__(self, sems, src, dst):
        f, c, _, _, _ = place()
        self.n = sems.take(8)
        self.sems, self.src, self.dst = sems, src, dst

    def copy(self, j):
        f, c, _, _, _ = place()
        dev = {"fsdp": c // 8, "ctx": 8 * f + j}
        return self.sems.remote(self.src(j), self.dst(), dev, self.n + j, self.n + c % 8)

    def start(self, only=range(8)):
        _, c, _, _, _ = place()
        for j in only:
            @pl.when(jnp.logical_not(jnp.logical_and(own_pair(), c % 8 == j)))
            def _():
                self.copy(j).start()

    def wait_recv(self):
        _, c, _, _, _ = place()
        for j in range(8):
            @pl.when(jnp.logical_not(jnp.logical_and(own_pair(), c % 8 == j)))
            def _():
                self.sems.remote(self.src(j), self.dst(), {"fsdp": 1 - place()[0]}, self.n, self.n + j).wait_recv()

    def wait_send(self):
        _, c, _, _, _ = place()
        for j in range(8):
            @pl.when(jnp.logical_not(jnp.logical_and(own_pair(), c % 8 == j)))
            def _():
                self.copy(j).wait_send()


class Sems:
    def __init__(self, send, recv):
        self.send, self.recv, self.n = send, recv, 0

    def take(self, n=1):
        first = self.n
        self.n += n
        return first

    def remote(self, src, dst, dev, i=None, recv_i=None):
        i = self.take() if i is None else i
        return pltpu.make_async_remote_copy(
            src_ref=src, dst_ref=dst, send_sem=self.send.at[i],
            recv_sem=self.recv.at[i if recv_i is None else recv_i],
            device_id=dev, device_id_type=MESH)

    def local(self, src, dst):
        return pltpu.make_async_copy(src, dst, self.send.at[self.take()])


def ctx_dev(y, x):
    return {"ctx": y * 4 + x}


class Gather2:
    def __init__(self, sems, buf, src, m, cut, order=None, first=0, width=None):
        _, _, _, y, x = place()
        self.sems, self.src = sems, src
        width = buf.shape[-1] if width is None else width
        cols = (pl.ds(first, width), pl.ds(first, cut), pl.ds(first + cut, width - cut))
        pick = lambda h: cols[0 if h is None else h + 1]
        if (m if order is None else order) == 0:
            r1, r2 = x, y
            self.dev1 = lambda i: ctx_dev(y, i)
            self.dev2 = lambda i: ctx_dev(i, x)
            self.slot = lambda i, h=None: buf.at[y, i, m, :, pick(h)]
            self.group = lambda i, h=None: buf.at[i, :, m, :, pick(h)]
        else:
            r1, r2 = y, x
            self.dev1 = lambda i: ctx_dev(i, x)
            self.dev2 = lambda i: ctx_dev(y, i)
            self.slot = lambda i, h=None: buf.at[i, x, m, :, pick(h)]
            self.group = lambda i, h=None: buf.at[:, i, m, :, pick(h)]
        self.n1 = (r1, (r1 + 1) % 4, (r1 + 3) % 4)
        self.n2 = (r2, (r2 + 1) % 4, (r2 + 3) % 4)
        self.keep = sems.local(src, self.slot(r1))
        self.sent = []

    def _go(self, src, dst, dev):
        c = self.sems.remote(src, dst, dev)
        c.start()
        self.sent.append(c)
        return c

    def s1(self):
        r = self.n1[0]
        self.keep.start()
        self.a = [self._go(self.src, self.slot(r), self.dev1((r + k) % 4)) for k in (1, 3, 2)]

    def s3(self):
        r, right, left = self.n2
        self.keep.wait()
        for c in self.a:
            c.wait_recv()
        self.c = [self._go(self.group(r), self.group(r), self.dev2(right)), self._go(self.group(r), self.group(r), self.dev2(left))]

    def s4(self):
        r, right, left = self.n2
        self.c[0].wait_recv()
        d0 = self._go(self.group(left, 0), self.group(left, 0), self.dev2(right))
        self.c[1].wait_recv()
        d1 = self._go(self.group(right, 1), self.group(right, 1), self.dev2(left))
        self.d = [d0, d1]

    def s5(self):
        self.d[0].wait_recv()
        self.d[1].wait_recv()

    def fin(self):
        for c in self.sent:
            c.wait_send()


def both(pair, step):
    for g in pair:
        getattr(g, step)()


class WeightGather:
    def __init__(self, sems, src, full, stride, first):
        f, _, t, _, _ = place()
        self.sems, self.src, self.f, self.t = sems, src, f, t
        rows = pl.ds(pl.multiple_of(f * 1024, 1024), 1024)
        top = pl.ds(pl.multiple_of(f * 1024, 1024), 512)
        low = pl.ds(pl.multiple_of(f * 1024 + 512, 512), 512)
        col = lambda z: pl.ds(pl.multiple_of(z * stride + first, 256), 256)
        self.part = lambda z, h=None: full.at[(rows, top, low)[0 if h is None else h + 1], col(z)]
        self.sent, self.crossed = [], []

    def _go(self, src, dst, dev):
        c = self.sems.remote(src, dst, dev)
        c.start()
        self.sent.append(c)
        return c

    def _cross(self, z, src=None):
        c = self._go(self.part(z) if src is None else src, self.part(z), {"fsdp": 1 - self.f})
        self.crossed.append(c)

    def s1(self):
        t = self.t
        self.keep = self.sems.local(self.src, self.part(t))
        self.keep.start()
        self.a = [self._go(self.src, self.part(t), {"tp": (t + 1) % 4}), self._go(self.src, self.part(t), {"tp": (t + 3) % 4})]

    def cross_own(self):
        self._cross(self.t, self.src)

    def s2(self):
        t = self.t
        right, left = (t + 1) % 4, (t + 3) % 4
        self.a[0].wait_recv()
        b0 = self._go(self.part(left, 0), self.part(left, 0), {"tp": right})
        self.a[1].wait_recv()
        b1 = self._go(self.part(right, 1), self.part(right, 1), {"tp": left})
        self.b = [b0, b1]
        self._cross(left)
        self._cross(right)

    def s3(self):
        self.b[0].wait_recv()
        self.b[1].wait_recv()
        self._cross((self.t + 2) % 4)

    def need(self, i):
        if i == 0:
            self.keep.wait()
        self.crossed[i].wait_recv()
        return (self.t + (0, 3, 1, 2)[i]) % 4

    def fin(self):
        for c in self.sent:
            c.wait_send()


def front_kernel(tok_in, router_in, gains_in, qk_in, routes_in, rope, cot, wqkv, wout, ein, eout,
                 wq_o, wo_o, sm_o, xc_o, p_o, oc_o, h1_o, qkv_r_o, of_o, e_o, rt_o, pr_o, y_o, gw_o, yr_o, dxe_o,
                 tok, rtr, gns, qkg_s, routes, wq, wo, tab, tab2, sm, xn1, p, oc, qkv_r, of, es, pr_s, h1_s,
                 qkvs, os, orr, att_s, att_r, msg, xg, cg, win, wdn, dhp, ab_s, g_s, dg_s, xcat, ccat, dab, gh, acc, dxb, yb, gw, dxe,
                 ssem, rsem, *rings):
    f, c, t, y, x = place()
    sems = Sems(ssem, rsem)
    partner = {"fsdp": 1 - f}
    half = pl.ds(pl.multiple_of(f * 1024, 1024), 1024)
    hello()
    first = [sems.local(gains_in, gns), sems.local(tok_in, tok), sems.local(router_in, rtr), sems.local(qk_in, qkg_s), sems.local(routes_in, routes),
             sems.local(rope.at[pl.ds(pl.multiple_of(c * 64, 64), 64)], tab)]
    own = []
    for k in (1, 2, 0):
        own.append(sems.local(wqkv.at[k], wq.at[half, pl.ds(512 * k, 512)]))
    own.append(sems.local(wout, wo.at[half]))
    for cp in first + own:
        cp.start()
    first[0].wait()
    first[1].wait()
    g_own = gns[0:1, :].astype(F32)
    r1 = []
    for z in range(4):
        for m in range(2):
            r1.append(inv_rms(tok[m, 16 * z:16 * z + 16, :].astype(F32)))
            v = tok[m, 16 * z:16 * z + 16, half].astype(F32)
            xn1[32 * z + 16 * m:32 * z + 16 * m + 16, half] = (v * r1[-1] * g_own).astype(BF)
    first[2].wait()
    first[3].wait()
    own_small = jnp.concatenate([rtr[...].astype(F32), gns[...].astype(F32), jnp.zeros((14, 1024), F32)], axis=0)
    sm[f] = own_small
    sm[f, 18:20, 0:64] = qkg_s[...].astype(F32)
    greeted()
    swap_small = sems.remote(sm.at[f], sm.at[f], partner)
    swap_small.start()
    weights = [WeightGather(sems, eout, wdn, 256, 0), WeightGather(sems, ein.at[0], win, 512, 0), WeightGather(sems, ein.at[1], win, 512, 256)]
    for w in weights[:2]:
        w.s1()
    swaps = []
    for k in (1, 2, 0):
        swaps.append(sems.remote(wqkv.at[k], wq.at[half, pl.ds(512 * k, 512)], partner))
    swaps.append(sems.remote(wout, wo.at[half], partner))
    for cp in swaps:
        cp.start()
    for w in weights[:2]:
        w.cross_own()
    rows16 = pl.ds(pl.multiple_of(t * 16, 16), 16)
    cots = [Gather2(sems, cg, cot.at[m, rows16], m, 1024) for m in range(2)]
    both(cots, "s1")

    lhs_own = xn1[:, half]
    for n, k in enumerate((1, 2, 0)):
        own[n].wait()
        p[k] = jnp.dot(lhs_own, wq[half, 512 * k:512 * k + 512], preferred_element_type=F32)
    for cp in first[4:]:
        cp.wait()
    for z in range(4):
        for m in range(2):
            tab2[32 * z + 16 * m:32 * z + 16 * m + 16, :] = tab[16 * z:16 * z + 16, :]
    swap_small.wait_recv()
    rest = pl.ds(pl.multiple_of((1 - f) * 1024, 1024), 1024)
    g_rest = sm[1 - f, 16:17, :]
    for z in range(4):
        for m in range(2):
            v = tok[m, 16 * z:16 * z + 16, rest].astype(F32)
            xn1[32 * z + 16 * m:32 * z + 16 * m + 16, rest] = (v * r1[2 * z + m] * g_rest).astype(BF)
    swap_x = sems.remote(xn1.at[:, rest], xc_o.at[1], partner)
    swap_x.start()
    g2 = jnp.concatenate([sm[0, 17:18, :], sm[1, 17:18, :]], axis=1)
    qkg = jnp.concatenate([sm[0, 18:20, 0:64], sm[1, 18:20, 0:64]], axis=1)
    cos, sin = tab2[:, :128], tab2[:, 128:]
    lhs_rest = xn1[:, rest]
    for n, k in enumerate((1, 2, 0)):
        swaps[n].wait_recv()
        pk = p[k] + jnp.dot(lhs_rest, wq[rest, 512 * k:512 * k + 512], preferred_element_type=F32)
        if k < 2:
            p[k] = pk
        for hl in range(4):
            u = pk[:, 128 * hl:128 * hl + 128]
            if k < 2:
                u = u * inv_rms(u) * qkg[k:k + 1]
                u = u * cos + pltpu.roll(u, 64, 1) * sin
            u = u.astype(BF)
            for m in range(2):
                for z in range(4):
                    qkvs[4 * m + hl, k, 16 * z:16 * z + 16, :] = u[32 * z + 16 * m:32 * z + 16 * m + 16, :]

    heads = Heads(sems, lambda j: qkvs.at[j], lambda: qkv_r.at[:, c])
    heads.start()

    @pl.when(own_pair())
    def _():
        qkv_r[:, c] = qkvs[c % 8]

    weights[0].s2()
    heads.wait_recv()
    mine8 = pl.ds(pl.multiple_of(8 * f, 8), 8)
    rest8 = pl.ds(pl.multiple_of(8 * (1 - f), 8), 8)
    swap_kv = sems.remote(qkv_r.at[pl.ds(1, 2), mine8], qkv_r.at[pl.ds(1, 2), mine8], partner)
    swap_kv.start()
    sums = []
    for part in range(2):
        at = (mine8, rest8)[part]
        if part == 1:
            swap_kv.wait_recv()
        keys = qkv_r[1, at].reshape(512, HD)
        vals = qkv_r[2, at].reshape(512, HD)
        for b in range(4):
            qb = qkv_r[0, pl.ds(8 * f + 2 * b, 2)].reshape(128, HD)
            e = jnp.exp(nt(qb, keys) * SCALE)
            total = jnp.sum(e, axis=1, keepdims=True)
            eb = e.astype(BF)
            ob = jnp.dot(eb, vals, preferred_element_type=F32)
            rows = slice(128 * b, 128 * b + 128)
            es[1 - part, rows, :] = eb
            if part == 0:
                sums.append(total)
                of[rows, :] = ob
            else:
                ri = 1.0 / (sums[b] + total)
                g_s[rows, :] = jnp.broadcast_to(ri, (128, 128))
                ob = (of[rows, :] + ob) * ri
                of[rows, :] = ob
                os[2 * b:2 * b + 2] = ob.astype(BF).reshape(2, 64, HD)
    o_back = Heads(sems, lambda j: os.at[j], lambda: orr.at[c % 8])
    o_back.start()
    both(cots, "s3")
    keep = [sems.local(wq, wq_o), sems.local(sm, sm_o), sems.local(xn1.at[:, half], xc_o.at[0]), sems.local(p.at[pl.ds(0, 2)], p_o), sems.local(qkv_r, qkv_r_o),
            sems.local(of, of_o), sems.local(es, e_o), sems.local(g_s, rt_o)]
    for cp in keep:
        cp.start()

    @pl.when(own_pair())
    def _():
        orr[c % 8] = os[c % 8]

    o_back.wait_recv()
    for j in range(8):
        m, hl = j // 4, j % 4
        for z in range(4):
            oc[0, 32 * z + 16 * m:32 * z + 16 * m + 16, 128 * hl:128 * hl + 128] = orr[j, 16 * z:16 * z + 16, :]

    own[3].wait()
    swaps[3].wait_recv()
    for n in range(4):
        part = nt(oc[0], wo[512 * n:512 * n + 512, :]).astype(BF)
        att_s[:, :, 512 * n:512 * n + 512] = part.reshape(4, 32, 512)
    a0 = sems.take(3)
    att_out = [sems.remote(att_s.at[(t + k) % 4], att_r.at[k - 1], {"tp": (t + k) % 4}, a0 + k - 1) for k in (1, 3, 2)]
    for cp in att_out:
        cp.start()
    weights[1].s2()
    swap_o = sems.remote(oc.at[0], oc.at[1], partner)
    swap_o.start()
    more = [sems.local(wo, wo_o)]
    more[0].start()
    both(cots, "s4")
    xq = jnp.concatenate([tok[m, rows16, :] for m in range(2)], axis=0).astype(F32)
    h1 = xq + att_s[t].astype(F32)
    for cp in att_out:
        cp.wait_recv()
    for k in range(3):
        h1 = h1 + att_r[k].astype(F32)
    weights[2].s1()
    weights[2].cross_own()
    h1_s[...] = h1
    xn2 = (h1 * inv_rms(h1) * g2).astype(BF)
    router = jnp.concatenate([sm[0, :16, :], sm[1, :16, :]], axis=1).astype(BF)
    logits = nt(xn2, router)
    e = jnp.exp(logits - jnp.max(logits, axis=1, keepdims=True))
    pr = e / jnp.sum(e, axis=1, keepdims=True)
    chosen = chosen_in(routes)
    gate = pr * chosen
    pr_s[0] = pr
    pr_s[1] = chosen
    ghi = gate.astype(BF)
    glo = (gate - ghi.astype(F32)).astype(BF)
    tail = jnp.concatenate([ghi, glo, jnp.zeros((32, 96), BF)], axis=1)
    for m in range(2):
        msg[m, :, :2048] = xn2[16 * m:16 * m + 16, :]
        msg[m, :, 2048:] = tail[16 * m:16 * m + 16, :]
    halves = ((0, 1024), (1024, 1152))
    gathers = [[Gather2(sems, xg, msg.at[m, :, pl.ds(first, width)], m, 512, h, first, width) for h, (first, width) in enumerate(halves)] for m in range(2)]
    both(gathers[0], "s1")
    both(gathers[1], "s1")
    more += [sems.local(h1_s, h1_o), sems.local(pr_s, pr_o)]
    for cp in more[-2:]:
        cp.start()
    both(cots, "s5")
    far = pl.ds(pl.multiple_of((1 - f) * 1024, 1024), 1024)
    pass_on = [sems.local(cg.at[:, :, :, :, half], ccat.at[0]), sems.remote(cg.at[:, :, :, :, far], ccat.at[1], partner)]
    for cp in pass_on:
        cp.start()
    swap_o.wait_recv()
    swap_x.wait_recv()
    more.append(sems.local(oc, oc_o))
    more[-1].start()
    both(gathers[0], "s3")
    weights[0].s3()
    both(gathers[1], "s3")

    for n in range(4):
        cols = pl.ds(pl.multiple_of(weights[0].need(n) * 256, 256), 256)
        v = jnp.dot(cg[...].reshape(512, 2048), wdn[:, cols], preferred_element_type=F32).reshape(4, 4, 2, 16, 256)
        for m in range(2):
            dhp[m, :, cols] = v[:, :, m].reshape(256, 256)
        if n == 1:
            both(gathers[0], "s4")
    weights[1].s3()
    both(gathers[1], "s4")
    both(gathers[0], "s5")

    lane = lax.broadcasted_iota(jnp.int32, (256, 128), 1)
    mine = jnp.logical_or(lane == c, lane == c + 16)
    keep[-1].wait()

    def open_gates(m):
        gates = xg[:, :, m, :, 2048:].reshape(256, 128).astype(F32)
        g_s[pl.ds(256 * m, 256), :] = jnp.broadcast_to(jnp.sum(jnp.where(mine, gates, 0.0), axis=1, keepdims=True), (256, 128))
        dg_s[pl.ds(256 * m, 256), :] = jnp.zeros((256, 128), F32)

    def hidden(n, m, z):
        cols = pl.ds(pl.multiple_of(z * 256, 256), 256)
        up = pl.multiple_of(z * 512, 512)
        ab_s[m] = jnp.dot(xg[:, :, m, :, :2048].reshape(256, 2048), win[:, pl.ds(up, 512)], preferred_element_type=F32)
        for i in range(4):
            rows = slice(64 * i, 64 * i + 64)
            both_rows = slice(256 * m + 64 * i, 256 * m + 64 * i + 64)
            a, b, dh, g = ab_s[m, rows, 0:256], ab_s[m, rows, 256:512], dhp[m, rows, cols], g_s[both_rows, 0:1]
            sg = jax.nn.sigmoid(a)
            act = a * sg
            hid = (act * b).astype(BF).astype(F32)
            prod = hid * dh
            dg_s[both_rows, :] = dg_s[both_rows, :] + prod[:, :128] + prod[:, 128:]
            gh[0, m, rows, cols] = (g * hid).astype(BF)
            dhid = g * dh
            dab[0, m, rows, pl.ds(up, 256)] = (dhid * b * sg * (1.0 + a * (1.0 - sg))).astype(BF)
            dab[0, m, rows, pl.ds(pl.multiple_of(up + 256, 256), 256)] = (dhid * act).astype(BF)
        for q in range(4):
            wide = slice(512 * q, 512 * q + 512)
            v = nt(dab[0, m, :, pl.ds(up, 512)], win[wide, pl.ds(up, 512)])
            keep_in = acc.at[m, :, wide] if q < 2 else gw.at[0, pl.ds(256 * m, 256), pl.ds(512 * q - 1024, 512)]
            if n > 0:
                v = v + keep_in[...].astype(F32)
            if n < 3:
                keep_in[...] = v.astype(keep_in.dtype)
            else:
                dxb[:, :, m, :, wide] = v.astype(BF).reshape(4, 4, 16, 512)

    rdx = []

    def send_dx(m):
        dgate = jnp.sum(dg_s[pl.ds(256 * m, 256), :], axis=1, keepdims=True)
        dhi = dgate.astype(BF).astype(F32)
        tail = jnp.where(lane == c, dhi, jnp.where(lane == c + 16, dgate - dhi, 0.0)).astype(BF)
        dxb[:, :, m, :, 2048:] = tail.reshape(4, 4, 16, 128)
        rdx.append([Scatter2(sems, dxb, m, 512, rings[8 * m + 4 * h:8 * m + 4 * h + 4], 16, h, first, width) for h, (first, width) in enumerate(halves)])
        both(rdx[m], "s1")

    def hand_over(z):
        for ref, at in ((dab, pl.ds(pl.multiple_of(z * 512, 512), 512)), (gh, pl.ds(pl.multiple_of(z * 256, 256), 256))):
            pass_on.append(sems.remote(ref.at[0, :, :, at], ref.at[1, :, :, at], partner))
            pass_on[-1].start()

    for n in range(4):
        if n == 3:
            weights[2].s3()
        z = weights[1].need(n)
        weights[2].need(n)
        for m in range(2):
            if n == 0:
                if m == 1:
                    weights[2].s2()
                    both(gathers[1], "s5")
                    pass_on += [sems.local(xg.at[:, :, :, :, half], xcat.at[0]), sems.remote(xg.at[:, :, :, :, far], xcat.at[1], partner)]
                    for cp in pass_on[2:]:
                        cp.start()
                open_gates(m)
            hidden(n, m, z)
            if n == 3:
                send_dx(m)
        hand_over(z)

    def grads(k, n):
        src = ccat if k == 2 else xcat
        rhs = gh[...].reshape(1024, 1024) if k == 2 else dab[:, :, :, 1024 * k:1024 * k + 1024].reshape(1024, 1024)
        at = slice(512 * n, 512 * n + 512)
        gw[k, at, :] = tn(jnp.concatenate([src[o, :, :, m, :, at].reshape(256, 512) for o in range(2) for m in range(2)], axis=0), rhs).astype(BF)

    def keep_grads(k):
        more.append(sems.local(gw.at[k], gw_o.at[k]))
        more[-1].start()

    def half_y(lo):
        for n in range(lo, lo + 2):
            cols = slice(512 * n, 512 * n + 512)
            v = nt(gh[0].reshape(512, 1024), wdn[cols, :]).astype(BF).reshape(2, 4, 4, 16, 512)
            for m in range(2):
                yb[:, :, m, :, cols] = v[m]

    half_y(0)
    both(rdx[0], "s2")
    half_y(2)
    more.append(sems.local(yb, y_o))
    more[-1].start()
    both(rdx[1], "s2")
    for cp in (pass_on[0], pass_on[2]):
        cp.wait()
    for cp in [pass_on[1]] + pass_on[3:]:
        cp.wait_recv()
    grads(0, 0)
    both(rdx[0], "s3")
    grads(0, 1)
    keep_grads(0)
    grads(1, 0)
    both(rdx[1], "s3")
    ry = [Scatter2(sems, yb, m, 1024, (yr_o.at[m, 0], yr_o.at[m, 1], None, None)) for m in range(2)]
    both(ry, "s1")
    grads(1, 1)
    keep_grads(1)
    grads(2, 0)
    grads(2, 1)
    keep_grads(2)
    both(cots, "fin")
    both(gathers[0] + gathers[1], "fin")
    for w in weights:
        w.fin()
    heads.wait_send()
    o_back.wait_send()
    for cp in keep[:-1]:
        cp.wait()
    for cp in swaps + [swap_small, swap_kv, swap_x, swap_o]:
        cp.wait_send()
    for cp in [pass_on[1]] + pass_on[3:]:
        cp.wait_send()
    for cp in att_out:
        cp.wait_send()
    for m in range(2):
        both(rdx[m], "s5")
        for h, (first, width) in enumerate(halves):
            dxe[16 * m:16 * m + 16, first:first + width] = rdx[m][h].result(pl.ds(0, 16))
    more.append(sems.local(dxe, dxe_o))
    more[-1].start()
    both(rdx[0] + rdx[1], "fin")
    for r in ry:
        for cp in r.a:
            cp.wait()
    for cp in more:
        cp.wait()


class GatherZ:
    def __init__(self, sems, buf):
        _, _, t, _, _ = place()
        self.sems, self.buf, self.t = sems, buf, t
        self.right, self.left = (t + 1) % 4, (t + 3) % 4
        self.sent = []

    def _go(self, ref, z):
        c = self.sems.remote(ref, ref, {"tp": z})
        c.start()
        self.sent.append(c)
        return c

    def s1(self):
        own = self.buf.at[self.t]
        self.a = [self._go(own, self.right), self._go(own, self.left)]

    def s2(self):
        self.a[0].wait_recv()
        b0 = self._go(self.buf.at[self.left, :, pl.ds(0, 1024)], self.right)
        self.a[1].wait_recv()
        self.b = [b0, self._go(self.buf.at[self.right, :, pl.ds(1024, 1024)], self.left)]

    def s3(self):
        for c in self.b:
            c.wait_recv()

    def fin(self):
        for c in self.sent:
            c.wait_send()


class SumZ:
    def __init__(self, sems, buf, ra, rb):
        _, _, t, _, _ = place()
        self.sems, self.buf, self.ra, self.rb = sems, buf, ra, rb
        self.n = (t, (t + 1) % 4, (t + 2) % 4, (t + 3) % 4)
        self.sent = []

    def _go(self, src, dst, z):
        c = self.sems.remote(src, dst, {"tp": z})
        c.start()
        self.sent.append(c)
        return c

    def s1(self):
        _, right, opp, left = self.n
        self.a = [self._go(self.buf.at[opp, :, pl.ds(1024 * h, 1024)], self.ra.at[h], z) for h, z in ((0, right), (1, left))]

    def s2(self):
        _, right, opp, left = self.n
        self.b = []
        for h, z in ((0, right), (1, left)):
            self.a[h].wait_recv()
            at = (z, slice(None), pl.ds(1024 * h, 1024))
            self.buf[at] = (self.buf[at].astype(F32) + self.ra[h].astype(F32)).astype(BF)
            self.b.append(self._go(self.buf.at[z], self.rb.at[h], z))

    def result(self):
        for c in self.b:
            c.wait_recv()
        return self.buf[self.n[0]].astype(F32) + self.rb[0].astype(F32) + self.rb[1].astype(F32)

    def fin(self):
        for c in self.sent:
            c.wait_send()


def chosen_in(routes):
    _, _, t, _, _ = place()
    expert = lax.broadcasted_iota(jnp.int32, (E, 64), 0)
    pick = (lax.broadcasted_iota(jnp.int32, (16, 64), 1) == 16 * t + lax.broadcasted_iota(jnp.int32, (16, 64), 0)).astype(F32).astype(BF)
    parts = []
    for m in range(2):
        hit = routes[m, 0:1, :] == expert
        for j in range(1, 8):
            hit = jnp.logical_or(hit, routes[m, j:j + 1, :] == expert)
        parts.append(nt(pick, hit.astype(F32).astype(BF)))
    return jnp.concatenate(parts, axis=0)


def rope_const():
    w = BASE ** (-(np.arange(64, dtype=np.float32) * np.float32(2.0) / np.float32(HD)))
    ang = np.arange(1024, dtype=np.float32)[:, None] * w.astype(np.float32)[None, :]
    cos, sin = np.cos(ang), np.sin(ang)
    return np.concatenate([cos, cos, -sin, sin], axis=1).astype(np.float32)


def front(tok, cot, wqkv, wout, small, ein, eout, routes):
    sd = jax.ShapeDtypeStruct
    v = pltpu.VMEM
    shapes = [
        sd((2048, 1536), BF), sd((2048, 512), BF), sd((2, 32, 1024), F32), sd((2, 128, 1024), BF), sd((2, 128, 512), F32),
        sd((2, 128, 512), BF), sd((32, 2048), F32), sd((3, 16, 64, HD), BF), sd((512, HD), F32),
        sd((2, 512, 512), BF), sd((512, 128), F32), sd((2, 32, 16), F32), sd((4, 4, 2, 16, 2048), BF), sd((3, 1024, 1024), BF), sd((2, 2, 4, 16, 1024), BF), sd((32, 2176), F32)]
    rings = []
    for width in (1024, 1152, 1024, 1152):
        rings += Scatter2.scratch(16, width, 512)
    outs = pl.pallas_call(
        front_kernel,
        out_shape=shapes,
        in_specs=[ANY] * 11,
        out_specs=[ANY] * 16,
        scratch_shapes=[
            v((2, 64, 2048), BF), v((16, 1024), BF), v((2, 1024), BF), v((2, 64), BF), v((2, 8, 64), jnp.int32),
            v((2048, 1536), BF), v((2048, 512), BF), v((64, 256), F32), v((128, 256), F32),
            v((2, 32, 1024), F32), v((128, 2048), BF), v((3, 128, 512), F32), v((2, 128, 512), BF), v((3, 16, 64, HD), BF), v((512, HD), F32),
            v((2, 512, 512), BF), v((2, 32, 16), F32), v((32, 2048), F32),
            v((8, 3, 64, HD), BF), v((8, 64, HD), BF), v((8, 64, HD), BF),
            v((4, 32, 2048), BF), v((3, 32, 2048), BF), v((2, 16, 2176), BF),
            v((4, 4, 2, 16, 2176), BF), v((4, 4, 2, 16, 2048), BF), v((2048, 2048), BF), v((2048, 1024), BF),
            v((2, 256, 1024), F32), v((2, 256, 512), F32), v((512, 128), F32), v((512, 128), F32),
            v((2, 4, 4, 2, 16, 1024), BF), v((2, 4, 4, 2, 16, 1024), BF), v((2, 2, 256, 2048), BF), v((2, 2, 256, 1024), BF), v((2, 256, 1024), F32),
            v((4, 4, 2, 16, 2176), BF), v((4, 4, 2, 16, 2048), BF), v((3, 1024, 1024), BF), v((32, 2176), F32),
            pltpu.SemaphoreType.DMA((192,)), pltpu.SemaphoreType.DMA((192,))] + rings,
        compiler_params=pltpu.CompilerParams(collective_id=0, has_side_effects=True, vmem_limit_bytes=62 << 20),
        name="front",
    )(tok, *small, routes, jnp.asarray(rope_const()), cot, wqkv, wout, ein, eout)
    names = ("wq", "wo", "sm", "xc", "p", "oc", "h1", "qkv_r", "of", "e", "rt", "pr", "y", "gw", "yr", "dxe")
    return dict(zip(names, outs))


def add_rows(n, rows, step, body):
    def outer(i, _):
        def inner(j, _):
            body(i, pl.ds(pl.multiple_of(j * step, step), step))
            return 0
        return lax.fori_loop(0, rows // step, inner, 0)
    lax.fori_loop(0, n, outer, 0)


class Scatter2:
    def __init__(self, sems, buf, m, cut, bufs, step=16, order=None, first=0, width=None):
        _, _, _, y, x = place()
        self.order = m if order is None else order
        self.a = None
        self.sems, self.buf, self.m, self.step = sems, buf, m, step
        self.rows, width = buf.shape[-2], buf.shape[-1] if width is None else width
        self.lo, self.hi, self.all = pl.ds(first, cut), pl.ds(first + cut, width - cut), pl.ds(first, width)
        self.ra_lo, self.ra_hi, self.rb, self.sb = bufs
        if self.order == 0:
            r1, r2 = y, x
            self.dev1, self.dev2 = (lambda i: ctx_dev(i, x)), (lambda i: ctx_dev(y, i))
        else:
            r1, r2 = x, y
            self.dev1, self.dev2 = (lambda i: ctx_dev(y, i)), (lambda i: ctx_dev(i, x))
        ring = lambda r: (r, (r + 1) % 4, (r + 2) % 4, (r + 3) % 4)
        self.n1, self.n2 = ring(r1), ring(r2)
        self.sent = []

    @staticmethod
    def scratch(rows, width, cut):
        return [pltpu.VMEM((4, rows, cut), BF), pltpu.VMEM((4, rows, width - cut), BF), pltpu.VMEM((2, 4, rows, width), BF),
                pltpu.VMEM((3, rows, width), BF)]

    def idx(self, g, s, rows, cols):
        return (g, s, self.m, rows, cols) if self.order == 0 else (s, g, self.m, rows, cols)

    def group(self, g, cols):
        return self.buf.at[self.idx(g, slice(None), slice(None), cols)]

    def slot(self, s, cols):
        return self.buf.at[self.idx(self.n1[0], s, slice(None), cols)]

    def _go(self, src, dst, dev):
        c = self.sems.remote(src, dst, dev)
        c.start()
        self.sent.append(c)
        return c

    def _acc(self, g, s, rows, cols, *terms):
        at = self.idx(g, s, rows, cols)
        total = self.buf[at].astype(F32)
        for v in terms:
            total = total + v.astype(F32)
        return at, total

    def s1(self):
        r, right, opp, left = self.n1
        self.a = [self._go(self.group(opp, self.lo), self.ra_lo, self.dev1(right)), self._go(self.group(opp, self.hi), self.ra_hi, self.dev1(left))]

    def s2(self):
        r, right, opp, left = self.n1
        self.b = []
        for n, (g, cols, ra) in enumerate(((right, self.lo, self.ra_lo), (left, self.hi, self.ra_hi))):
            if self.a:
                self.a[n].wait_recv()

            def body(i, rows):
                at, total = self._acc(g, i, rows, cols, ra[i, rows, :])
                self.buf[at] = total.astype(BF)
            add_rows(4, self.rows, self.step, body)
            self.b.append(self._go(self.group(g, self.all), self.rb.at[n], self.dev1(g)))

    def s3(self):
        for cp in self.b:
            cp.wait_recv()

        def body(i, rows):
            at, total = self._acc(self.n1[0], i, rows, self.all, self.rb[0, i, rows, :], self.rb[1, i, rows, :])
            self.buf[at] = total.astype(BF)
        add_rows(4, self.rows, self.step, body)
        self.c = [self._go(self.slot(self.n2[k], self.all), self.sb.at[k - 1], self.dev2(self.n2[k])) for k in (1, 3, 2)]

    def s5(self):
        for cp in self.c:
            cp.wait_recv()

    def result(self, rows):
        return self._acc(self.n1[0], self.n2[0], rows, self.all, *[self.sb[k, rows, :] for k in range(3)])[1]

    def fin(self):
        for c in self.sent:
            c.wait_send()


class ScatterZ:
    def __init__(self, sems, view, ra, rb):
        _, _, t, _, _ = place()
        self.sems, self.view, self.ra, self.rb = sems, view, ra, rb
        self.n = (t, (t + 1) % 4, (t + 2) % 4, (t + 3) % 4)
        self.sent = []

    @staticmethod
    def scratch(width):
        return [pltpu.VMEM((2, 1024, width // 2), BF), pltpu.VMEM((2, 1024, width), BF)]

    def _go(self, src, dst, z):
        c = self.sems.remote(src, dst, {"tp": z})
        c.start()
        self.sent.append(c)
        return c

    def s1(self):
        r, right, opp, left = self.n
        self.a = [self._go(self.view(opp, h), self.ra.at[h], z) for h, z in ((0, right), (1, left))]

    def s2(self):
        r, right, opp, left = self.n
        self.b = []
        for h, z in ((0, right), (1, left)):
            self.a[h].wait_recv()
            half = self.view(z, h)

            def body(i, rows):
                half[rows, :] = (half[rows, :].astype(F32) + self.ra[h, rows, :].astype(F32)).astype(BF)
            add_rows(1, 1024, 64, body)
            self.b.append(self._go(self.view(z), self.rb.at[h], z))

    def s3(self, put):
        for cp in self.b:
            cp.wait_recv()
        mine = self.view(self.n[0])

        def body(i, rows):
            put(rows, (mine[rows, :].astype(F32) + self.rb[0, rows, :].astype(F32) + self.rb[1, rows, :].astype(F32)).astype(BF))
        add_rows(1, 1024, 64, body)

    def fin(self):
        for c in self.sent:
            c.wait_send()


class SumPlane:
    def __init__(self, sems, src, landing):
        _, _, _, y, x = place()
        self.src, self.landing = src, landing
        n = sems.take(6)
        self.step = [[sems.remote(src.at[a], landing.at[a, k - 1], ctx_dev(y, (x + k) % 4) if a == 0 else ctx_dev((y + k) % 4, x), n + 3 * a + k - 1)
                      for k in (1, 3, 2)] for a in range(2)]

    def start(self, a):
        for cp in self.step[a]:
            cp.start()

    def sum(self, a):
        for cp in self.step[a]:
            cp.wait_recv()
        total = self.src[a].astype(F32)
        for k in range(3):
            total = total + self.landing[a, k].astype(F32)
        return total

    def fin(self):
        for cp in self.step[0] + self.step[1]:
            cp.wait_send()


def back_kernel(dxe_in, tok_in, cot_in, pr_in, sm_in, xc_in, p_in, oc_in, h1_in, qkv_r_in, of_in, e_in, rt_in, rope, y_in, gw_in, yr_in, wq_in, wo_in,
                lay_o, gt_o, gall_o, sg_o, ge_o, g1_o,
                sg, g1f, dxe, lay, gt, ge, tok, cot, prs, sm, xc, p, oc, h1, qkv_r, of, rinv,
                wq, wo, tab, tab2, gw, yb, yr, pm, dA, do_s, do_r, dkv_o, dkv_p, bv_s, bv_r, bqk_s, bqk_r, gall, du, dp, dx1_s, dx1_a, dx1_b,
                dAc, ar, chunk, part, part_s, part_r, part_z, part_zr, part_c, part_cr, g1_s, g1_r, g1_z, ssem, rsem, *rings):
    f, c, t, y, x = place()
    hello()
    sems = Sems(ssem, rsem)
    partner = {"fsdp": 1 - f}
    rows16 = pl.ds(pl.multiple_of(t * 16, 16), 16)
    pairs = [(dxe_in, dxe), (h1_in, h1), (cot_in.at[:, rows16], cot), (pr_in, prs), (sm_in, sm), (y_in, yb), (yr_in, yr), (wo_in, wo), (qkv_r_in, qkv_r), (of_in, of),
             (e_in, pm), (rt_in, rinv), (oc_in, oc), (rope.at[pl.ds(pl.multiple_of(c * 64, 64), 64)], tab), (gw_in, gw), (p_in, p), (xc_in, xc),
             (wq_in, wq), (tok_in.at[:, rows16], tok)]
    load = [sems.local(*pair) for pair in pairs]
    for cp in load:
        cp.start()
    ry = [Scatter2(sems, yb, m, 1024, (yr.at[m, 0], yr.at[m, 1]) + tuple(rings[4 * m + 2:4 * m + 4])) for m in range(2)]
    rar = [[Scatter2(sems, ar.at[k], m, 256, rings[8 * k + 8 + 4 * m:8 * k + 12 + 4 * m], 32) for m in range(2)] for k in range(4)]

    def wide(z, h=None):
        first = (z % 2) * 512 + (0 if h is None else 256 * h)
        return gw.at[z // 2, :, pl.ds(pl.multiple_of(first, 256), 512 if h is None else 256)]

    def narrow(z, h=None):
        first = z * 256 + (0 if h is None else 128 * h)
        return gw.at[2, :, pl.ds(pl.multiple_of(first, 128), 256 if h is None else 128)]

    rz = [ScatterZ(sems, wide, *rings[40:42]), ScatterZ(sems, narrow, *rings[42:44])]
    for cp in load[:5]:
        cp.wait()
    g1 = jnp.concatenate([sm[0, 16:17, :], sm[1, 16:17, :]], axis=1)
    g2 = jnp.concatenate([sm[0, 17:18, :], sm[1, 17:18, :]], axis=1)
    qkg = jnp.concatenate([sm[0, 18:20, 0:64], sm[1, 18:20, 0:64]], axis=1)
    router = jnp.concatenate([sm[0, :16, :], sm[1, :16, :]], axis=1).astype(BF)
    hv = h1[...]
    r2 = inv_rms(hv)
    xn2 = (hv * r2 * g2).astype(BF)
    pr, chosen = prs[0], prs[1]
    cq = cot[...].reshape(32, 2048).astype(F32)
    got = dxe[...]
    dpr = chosen * (got[:, 2048:2064] + got[:, 2064:2080])
    dl = (pr * (dpr - jnp.sum(pr * dpr, axis=1, keepdims=True))).astype(BF)
    du2 = got[:, :2048] + jnp.dot(dl, router, preferred_element_type=F32)
    gdu = g2 * du2
    dh1 = cq + r2 * gdu - r2 * r2 * r2 * hv * jnp.mean(hv * gdu, axis=1, keepdims=True)
    dA[t] = dh1.astype(BF)
    greeted()
    d0 = sems.take(3)
    dA_out = [sems.remote(dA.at[t], dA.at[t], {"tp": (t + k) % 4}, d0 + k - 1) for k in (1, 3, 2)]
    for cp in dA_out:
        cp.start()
    load[5].wait()
    load[6].wait()
    both(ry, "s2")
    load[13].wait()
    for z in range(4):
        for m in range(2):
            tab2[32 * z + 16 * m:32 * z + 16 * m + 16, :] = tab[16 * z:16 * z + 16, :]
    g_router = tn(dl, xn2)
    g_g2 = jnp.sum(du2 * hv * r2, axis=0, keepdims=True)
    for h in range(2):
        cols = slice(1024 * h, 1024 * h + 1024)
        part[h] = jnp.zeros((32, 1024), F32)
        part[h, 0:16, :] = g_router[:, cols]
        part[h, 17:18, :] = g_g2[:, cols]
    load[7].wait()
    for cp in dA_out:
        cp.wait_recv()
    dA2 = dA[...].reshape(128, 2048)
    fo = pl.multiple_of((1 - f) * 1024, 1024)
    fm = pl.multiple_of(f * 1024, 1024)
    swap_a = sems.remote(dA.at[:, :, pl.ds(fo, 1024)], dAc.at[1], partner)
    swap_a.start()
    dd = jnp.dot(dA2, wo[...], preferred_element_type=F32).astype(BF)
    for hl in range(4):
        for m in range(2):
            for z in range(4):
                do_s[4 * m + hl, 16 * z:16 * z + 16, :] = dd[32 * z + 16 * m:32 * z + 16 * m + 16, 128 * hl:128 * hl + 128]
    do_out = Heads(sems, lambda j: do_s.at[j], lambda: do_r.at[c % 8])
    do_out.start()

    @pl.when(own_pair())
    def _():
        do_r[c % 8] = do_s[c % 8]

    both(ry, "s3")

    def grads(lhs, rhs, k):
        for n in range(2):
            v = tn(lhs[:, 512 * n:512 * n + 512], rhs).astype(BF)
            ar[k, 2 * n:2 * n + 2] = v.reshape(2, 4, 2, 32, 512)
        both(rar[k], "s1")

    load[14].wait()
    both(rz, "s1")
    dAc[0] = dA[:, :, pl.ds(fm, 1024)]
    load[12].wait()
    mine8 = pl.ds(pl.multiple_of(8 * f, 8), 8)
    rest8 = pl.ds(pl.multiple_of(8 * (1 - f), 8), 8)
    for cp in load[8:12]:
        cp.wait()
    keys = [qkv_r[1, at].reshape(512, HD) for at in (rest8, mine8)]
    vals = [qkv_r[2, at].reshape(512, HD) for at in (rest8, mine8)]
    queries = qkv_r[0, mine8].reshape(512, HD)
    swap_a.wait_recv()
    grads(dAc[...].reshape(256, 1024), oc[...].reshape(256, 512), 3)
    do_out.wait_recv()

    do_all = do_r[...].reshape(512, HD).astype(F32)
    ri = rinv[:, 0:1]
    scaled = (do_all * ri).astype(BF)
    dkv_o[1] = tn(pm[0], scaled).astype(BF)
    swap_v = sems.remote(dkv_o.at[1], dkv_p.at[1], partner)
    swap_v.start()
    dv = tn(pm[1], scaled)
    delta = ri * jnp.sum(do_all * of[...], axis=1, keepdims=True)
    for hk in range(2):
        dS = (pm[hk].astype(F32) * (nt(scaled, vals[hk]) - delta)).astype(BF)
        dk = tn(dS, queries)
        d = jnp.dot(dS, keys[hk], preferred_element_type=F32)
        dq = d if hk == 0 else dq + d
        if hk == 0:
            dkv_o[0] = (dk * SCALE).astype(BF)
            swap_k = sems.remote(dkv_o.at[0], dkv_p.at[0], partner)
            swap_k.start()
            swap_v.wait_recv()
            bv_s[...] = (dv + dkv_p[1].astype(F32)).astype(BF).reshape(8, 64, HD)
            v_out = Heads(sems, lambda j: bv_s.at[j], lambda: bv_r.at[c % 8])
            v_out.start()

            @pl.when(own_pair())
            def _():
                bv_r[c % 8] = bv_s[c % 8]
            both(rar[3], "s2")
    bqk_s[:, 0] = (dq * SCALE).astype(BF).reshape(8, 64, HD)
    swap_k.wait_recv()
    bqk_s[:, 1] = (dk * SCALE + dkv_p[0].astype(F32)).astype(BF).reshape(8, 64, HD)
    qk_out = Heads(sems, lambda j: bqk_s.at[j], lambda: bqk_r.at[c % 8])
    qk_out.start()

    @pl.when(own_pair())
    def _():
        bqk_r[c % 8] = bqk_s[c % 8]

    for cp in load[15:19]:
        cp.wait()
    v_out.wait_recv()
    for j in range(8):
        m, hl = j // 4, j % 4
        for z in range(4):
            dp[0, 32 * z + 16 * m:32 * z + 16 * m + 16, 1024 + 128 * hl:1024 + 128 * hl + 128] = bv_r[j, 16 * z:16 * z + 16, :]
    swap_d = {}

    def share(k):
        at = pl.ds(512 * k, 512)
        swap_d[k] = sems.remote(dp.at[0, :, at], dp.at[1, :, at], partner)
        swap_d[k].start()

    def qkv_grads(k):
        swap_d[k].wait_recv()
        grads(xc[...].reshape(256, 1024), dp[:, :, 512 * k:512 * k + 512].reshape(256, 512), k)

    gat = {}

    def publish(k):
        both(rar[k], "s5")
        gat[k] = []
        for m in range(2):
            chunk[k, m] = rar[k][m].result(pl.ds(0, 32)).astype(BF)
            gat[k].append(Gather2(sems, gall.at[k], chunk.at[k, m], m, 256))
        both(gat[k], "s1")

    def dxn1_part(n):
        cols = slice(512 * n, 512 * n + 512)
        dx1_s[:, :, cols] = nt(dp[0], wq[cols, :]).astype(BF).reshape(4, 32, 512)

    cos, sin = tab2[:, :128], tab2[:, 128:]

    def head_back(k):
        total = jnp.zeros((1, HD), F32)
        for hl in range(4):
            cols = slice(128 * hl, 128 * hl + 128)
            u = du[k, :, cols]
            u = u * cos - pltpu.roll(u, 64, 1) * sin
            pk = p[k, :, cols]
            r = inv_rms(pk)
            gu = qkg[k:k + 1] * u
            dp[0, :, 512 * k + 128 * hl:512 * k + 128 * hl + 128] = (r * gu - r * r * r * pk * jnp.mean(pk * gu, axis=1, keepdims=True)).astype(BF)
            total = total + jnp.sum(u * pk * r, axis=0, keepdims=True)
        share(k)
        part[0, 18 + k:19 + k, 0:64] = total[:, 0:64]
        part[1, 18 + k:19 + k, 0:64] = total[:, 64:128]

    share(2)
    both(rar[3], "s3")
    qkv_grads(2)
    rz[0].s2()
    qk_out.wait_recv()
    for j in range(8):
        m, hl = j // 4, j % 4
        for z in range(4):
            rows, src = slice(32 * z + 16 * m, 32 * z + 16 * m + 16), slice(16 * z, 16 * z + 16)
            for k in range(2):
                du[k, rows, 128 * hl:128 * hl + 128] = bqk_r[j, k, src, :].astype(F32)
    head_back(0)
    both(rar[2], "s2")
    head_back(1)
    qkv_grads(0)
    qkv_grads(1)
    part_s[...] = part[1 - f].astype(BF)
    swap_p = sems.remote(part_s, part_r, partner)
    swap_p.start()
    publish(3)
    both(rar[2], "s3")
    both(rar[0], "s2")
    dxn1_part(0)
    both(rar[1], "s2")
    dxn1_part(1)
    both(gat[3], "s3")
    publish(2)
    dxn1_part(2)
    both(rar[0], "s3")
    dxn1_part(3)
    dx1 = SumZ(sems, dx1_s, dx1_a, dx1_b)
    dx1.s1()
    both(rar[1], "s3")
    swap_p.wait_recv()
    total = (part[f] + part_r[...].astype(F32)).astype(BF)
    for z in range(4):
        part_z[z] = total[:, 256 * z:256 * z + 256]
    z0 = sems.take(3)
    pz_out = [sems.remote(part_z.at[(t + k) % 4], part_zr.at[k - 1], {"tp": (t + k) % 4}, z0 + k - 1) for k in range(1, 4)]
    for cp in pz_out:
        cp.start()
    both(gat[2], "s3")
    publish(0)
    both(gat[3], "s4")
    publish(1)
    dx1.s2()
    both(ry, "s5")
    mix = jnp.concatenate([ry[m].result(pl.ds(0, 16)) for m in range(2)], axis=0)
    lay[t] = (hv + mix).astype(BF)
    lay_all = GatherZ(sems, lay)
    lay_all.s1()
    both(gat[2], "s4")
    both(gat[0], "s3")
    tot = part_z[t].astype(F32)
    for k in range(3):
        pz_out[k].wait_recv()
        tot = tot + part_zr[k].astype(F32)
    part_c[0] = tot.astype(BF)
    small_sum = SumPlane(sems, part_c, part_cr)
    small_sum.start(0)
    both(gat[1], "s3")
    xv = tok[...].reshape(32, 2048).astype(F32)
    r1 = inv_rms(xv)
    dxn1 = dx1.result()
    gdu = g1 * dxn1
    gtv = dh1 + r1 * gdu - r1 * r1 * r1 * xv * jnp.mean(xv * gdu, axis=1, keepdims=True)
    gt[t] = gtv.astype(BF)
    gt_all = GatherZ(sems, gt)
    gt_all.s1()
    g_g1 = jnp.sum(dxn1 * xv * r1, axis=0, keepdims=True)
    for i in range(16):
        g1_s[0, i // 8, i % 8:i % 8 + 1, :] = g_g1[:, 128 * i:128 * i + 128]
    gain_sum = SumPlane(sems, g1_s, g1_r)
    gain_sum.start(0)
    rz[1].s2()
    both(gat[0], "s4")
    part_c[1] = small_sum.sum(0).astype(BF)
    small_sum.start(1)
    lay_all.s2()
    both(gat[2], "s5")
    both(gat[3], "s5")
    out_all = [sems.local(gall.at[k], gall_o.at[k]) for k in (2, 3)]
    for cp in out_all:
        cp.start()
    both(gat[1], "s4")
    g1_s[1] = gain_sum.sum(0)
    gain_sum.start(1)
    gt_all.s2()
    for cp in dA_out:
        cp.wait_send()
    for h in (do_out, v_out, qk_out):
        h.wait_send()
    for cp in [swap_d[k] for k in range(3)] + [swap_a, swap_p, swap_v, swap_k]:
        cp.wait_send()
    sg[t] = small_sum.sum(1)
    g0 = sems.take(3)
    sg_out = [sems.remote(sg.at[t], sg.at[t], {"tp": (t + k) % 4}, g0 + k - 1) for k in range(1, 4)]
    for cp in sg_out:
        cp.start()
    both(ry, "fin")
    for k in range(4):
        both(rar[k], "fin")
    tot = gain_sum.sum(1)
    g1_s[2] = tot
    b0 = sems.take(8)
    gb_out = []
    for k in range(1, 8):
        other, z = (f + k // 4) % 2, (t + k) % 4
        gb_out.append(sems.remote(g1_s.at[2], g1_z.at[f * 4 + t], {"fsdp": other, "tp": z}, b0 + k, b0 + (k if k < 4 else 4 + (8 - k) % 4)))
    for cp in gb_out:
        cp.start()
    g1_z[f * 4 + t] = tot

    def put_wide(rows, v):
        ge[0, rows, :] = v[:, :256]
        ge[1, rows, :] = v[:, 256:]

    def put_narrow(rows, v):
        ge[2, rows, :] = v

    rz[0].s3(put_wide)
    lay_all.s3()
    for src, dst in ((ge.at[pl.ds(0, 2)], ge_o.at[pl.ds(0, 2)]), (lay, lay_o)):
        out_all.append(sems.local(src, dst))
        out_all[-1].start()
    for k in (0, 1):
        both(gat[k], "s5")
        out_all.append(sems.local(gall.at[k], gall_o.at[k]))
        out_all[-1].start()
    gt_all.s3()
    out_all.append(sems.local(gt, gt_o))
    out_all[-1].start()
    rz[1].s3(put_narrow)
    out_all.append(sems.local(ge.at[2], ge_o.at[2]))
    out_all[-1].start()
    for cp in gb_out:
        cp.wait_recv()
    tot = g1_z[0]
    for k in range(1, 8):
        tot = tot + g1_z[k]
    g1f[...] = jnp.where(f == 0, tot[0], tot[1])
    for cp in sg_out:
        cp.wait_recv()
    for src, dst in ((g1f, g1_o), (sg, sg_o)):
        out_all.append(sems.local(src, dst))
        out_all[-1].start()

    both((dx1, lay_all, gt_all, small_sum, gain_sum), "fin")
    for g in [rz] + [gat[k] for k in range(4)]:
        both(g, "fin")
    for cp in pz_out + sg_out + gb_out:
        cp.wait_send()
    for cp in out_all:
        cp.wait()


def finish_kernel(lay, gt, gall, sg, ge, g1, lo_o, gt_o, gq_o, go_o, gg_o, gk_o, gr_o, gi_o, gd_o, *s):
    (lay_v, gt_v, gall_v, sg_v, ge_v, g1_v, lo_w, gt_w, gall_w, gg_w, gk_w, gr_w, ge_w, sem) = s
    i = 0

    def copy(src, dst):
        nonlocal i
        cp = pltpu.make_async_copy(src, dst, sem.at[i])
        i += 1
        cp.start()
        return cp

    get = [copy(gall.at[k], gall_v.at[k]) for k in range(4)] + [copy(ge.at[k], ge_v.at[k]) for k in range(3)]
    get += [copy(gt, gt_v), copy(lay, lay_v), copy(sg, sg_v), copy(g1, g1_v)]
    put = []
    for k in range(4):
        get[k].wait()

        def body(j, _):
            rows = pl.ds(pl.multiple_of(j * 64, 64), 64)
            gall_w[k, rows, :] = gall_v[k, rows, :].astype(F32)
            return 0
        lax.fori_loop(0, 16, body, 0)
        put.append(copy(gall_w.at[k], gq_o.at[k] if k < 3 else go_o))
    for k in range(3):
        get[4 + k].wait()

        def body(j, _):
            rows = pl.ds(pl.multiple_of(j * 128, 128), 128)
            ge_w[k, rows, :] = ge_v[k, rows, :].astype(F32)
            return 0
        lax.fori_loop(0, 8, body, 0)
        put.append(copy(ge_w.at[k], gi_o.at[0, k] if k < 2 else gd_o.at[0]))
    get[7].wait()
    get[8].wait()
    for z in range(4):
        for m in range(2):
            gt_w[m, 16 * z:16 * z + 16, :] = gt_v[z, 16 * m:16 * m + 16, :].astype(F32)
            lo_w[m, 16 * z:16 * z + 16, :] = lay_v[z, 16 * m:16 * m + 16, :]
    put += [copy(gt_w, gt_o.at[:, 0]), copy(lo_w, lo_o.at[:, 0])]
    get[9].wait()
    for z in range(4):
        cols = slice(256 * z, 256 * z + 256)
        gr_w[:, cols] = sg_v[z, 0:16, :]
        gg_w[1:2, cols] = sg_v[z, 17:18, :]
    get[10].wait()
    for i8 in range(8):
        gg_w[0:1, 128 * i8:128 * i8 + 128] = g1_v[i8:i8 + 1, :]
    gk_w[...] = sg_v[0, 18:20, 0:64]
    put += [copy(gr_w, gr_o), copy(gg_w, gg_o), copy(gk_w, gk_o)]
    for cp in put:
        cp.wait()


def finish(lay, gt, gall, sg, ge, g1):
    sd = jax.ShapeDtypeStruct
    v = pltpu.VMEM
    return pl.pallas_call(
        finish_kernel,
        out_shape=[sd((2, 1, 64, 2048), BF), sd((2, 1, 64, 2048), F32), sd((3, 1024, 512), F32), sd((1024, 512), F32),
                   sd((2, 1024), F32), sd((2, 64), F32), sd((16, 1024), F32), sd((1, 2, 1024, 256), F32), sd((1, 1024, 256), F32)],
        in_specs=[ANY] * 6,
        out_specs=[ANY] * 9,
        scratch_shapes=[
            v((4, 32, 2048), BF), v((4, 32, 2048), BF), v((4, 1024, 512), BF), v((4, 32, 256), F32), v((3, 1024, 256), BF), v((8, 128), F32),
            v((2, 64, 2048), BF), v((2, 64, 2048), F32), v((4, 1024, 512), F32), v((2, 1024), F32), v((2, 64), F32), v((16, 1024), F32),
            v((3, 1024, 256), F32), pltpu.SemaphoreType.DMA((24,))],
        compiler_params=pltpu.CompilerParams(vmem_limit_bytes=62 << 20),
        name="finish",
    )(lay, gt, gall.reshape(4, 1024, 512), sg, ge, g1)


def back(tok, cot, fr):
    sd = jax.ShapeDtypeStruct
    v = pltpu.VMEM
    rings = []
    for _ in range(2):
        rings += Scatter2.scratch(16, 2048, 1024)
    for _ in range(8):
        rings += Scatter2.scratch(32, 512, 256)
    rings += ScatterZ.scratch(512) + ScatterZ.scratch(256)
    outs = pl.pallas_call(
        back_kernel,
        out_shape=[sd((4, 32, 2048), BF), sd((4, 32, 2048), BF), sd((4, 4, 4, 2, 32, 512), BF), sd((4, 32, 256), F32), sd((3, 1024, 256), BF), sd((8, 128), F32)],
        in_specs=[ANY] * 19,
        out_specs=[ANY] * 6,
        scratch_shapes=[
            v((4, 32, 256), F32), v((8, 128), F32),
            v((32, 2176), F32), v((4, 32, 2048), BF), v((4, 32, 2048), BF), v((3, 1024, 256), BF),
            v((2, 16, 2048), BF), v((2, 16, 2048), BF), v((2, 32, 16), F32), v((2, 32, 1024), F32), v((2, 128, 1024), BF), v((2, 128, 512), F32),
            v((2, 128, 512), BF), v((32, 2048), F32), v((3, 16, 64, HD), BF), v((512, HD), F32), v((512, 128), F32),
            v((2048, 1536), BF), v((2048, 512), BF), v((64, 256), F32), v((128, 256), F32), v((3, 1024, 1024), BF),
            v((4, 4, 2, 16, 2048), BF), v((2, 2, 4, 16, 1024), BF), v((2, 512, 512), BF), v((4, 32, 2048), BF),
            v((8, 64, HD), BF), v((8, 64, HD), BF), v((2, 512, HD), BF), v((2, 512, HD), BF), v((8, 64, HD), BF), v((8, 64, HD), BF), v((8, 2, 64, HD), BF), v((8, 2, 64, HD), BF),
            v((4, 4, 4, 2, 32, 512), BF),
            v((2, 128, 512), F32), v((2, 128, 1536), BF), v((4, 32, 2048), BF), v((2, 32, 1024), BF), v((2, 32, 2048), BF),
            v((2, 4, 32, 1024), BF), v((4, 4, 4, 2, 32, 512), BF), v((4, 2, 32, 512), BF),
            v((2, 32, 1024), F32), v((32, 1024), BF), v((32, 1024), BF), v((4, 32, 256), BF), v((3, 32, 256), BF),
            v((2, 32, 256), BF), v((2, 3, 32, 256), BF),
            v((3, 2, 8, 128), F32), v((2, 3, 2, 8, 128), F32), v((8, 2, 8, 128), F32),
            pltpu.SemaphoreType.DMA((304,)), pltpu.SemaphoreType.DMA((304,))] + rings,
        compiler_params=pltpu.CompilerParams(collective_id=1, has_side_effects=True, vmem_limit_bytes=62 << 20),
        name="back",
    )(fr["dxe"], tok, cot, fr["pr"], fr["sm"], fr["xc"], fr["p"], fr["oc"], fr["h1"], fr["qkv_r"], fr["of"], fr["e"], fr["rt"], jnp.asarray(rope_const()),
      fr["y"], fr["gw"], fr["yr"], fr["wq"], fr["wo"])
    return finish(*outs)


def local(tokens, routes, cotangent, qkv_weight, out_weight, norm_gains, qk_gains, router_weight, expert_in, expert_out):
    tok = tokens.reshape(2, 64, 2048)
    cot = cotangent.reshape(2, 64, 2048)
    small = (router_weight, norm_gains, qk_gains)
    routes = jnp.swapaxes(routes.reshape(2, 64, 8), 1, 2)
    fr = front(tok, cot, qkv_weight, out_weight, small, expert_in[0], expert_out[0], routes)
    return tuple(back(tok, cot, fr))


def solution(mesh):
    act = P(None, "fsdp", "ctx", None)
    weights = (P(None, "fsdp", "tp"), P("fsdp", "tp"), P(None, "fsdp"), P(None, "fsdp"), P(None, "fsdp"), P("ctx", None, "fsdp", "tp"), P("ctx", "fsdp", "tp"))
    return jax.shard_map(local, mesh=mesh, in_specs=(act, act, act) + weights, out_specs=(act, act) + weights, check_vma=False)
```

time: 1650 us -> 196 us (0.12)
  waiting for transfers between devices: 1030 us -> 0 us
  local copies, waits for them, and re-layouts: 229 us -> 0 us
  Pallas kernels: 0 us -> 195 us
  blocking collectives: 136 us -> 0 us
  matrix products: 113 us -> 0 us
  other arithmetic: 71.2 us -> 0 us
  starting transfers between devices: 45.7 us -> 0 us
  between operations: 17.5 us -> 0.86 us
    all_to_all x7 -> x0, waiting for transfers between devices: 327 us -> none  [the longest x2 155 us: local(): lax.all_to_all(rows_grad, 'ctx', split_axis=1, concat_axis=0, tiled=True)]
    reduce_scatter x12 -> x0, waiting for transfers between devices: 295 us -> none  [the longest x2 149 us: local(): lax.psum_scatter(key_grads_all.astype(jnp.bfloat16), 'ctx', scatter_dimen...]
    pallas_call x0 -> x3, Pallas kernels: none -> 195 us  [the longest x1 98.6 us: front(): pl.pallas_call(front_kernel, out_shape=shapes, in_specs=[ANY] * 11, out_s...]
    all_gather x8 -> x0, waiting for transfers between devices: 185 us -> none  [the longest x2 84.7 us: local(): lax.all_gather(value_local, 'ctx', axis=1, tiled=True)]
    unnamed x34 -> x0, waiting for transfers between devices: 124 us -> none
    dot_general x42 -> x0, matrix products: 113 us -> none  [the longest x2 11 us: local(): jnp.einsum('krh,kdh->rd', proj_grad, qkv_back, preferred_element_type=jnp...]
    scatter x4 -> x0, local copies, waits for them, and re-layouts: 102 us -> none  [the longest x2 51.7 us: slot_tables(): filled = jnp.zeros((expert_count, seq_count, capacity), jnp.bool_).at[rou...]
    psum x4 -> x0, waiting for transfers between devices: 98.4 us -> none  [the longest x1 44.4 us: local(): lax.psum(running[0].astype(jnp.bfloat16), 'ctx').astype(jnp.float32)]
  transfers between devices with their start and end apart: 36 -> 0, of which waited for: 34 -> 0; matrix products, arithmetic and copies ran while one was open for 19% -> 0% of each run, Pallas kernels for 0% -> 0%
where the time goes in v1:
time: 196 us
  Pallas kernels  195 us (99%)
    pallas_call x1, Pallas kernels, front(): pl.pallas_call(front_kernel, out_shape=shapes, in_specs=[ANY] * 11, out_s...  98.6 us
    pallas_call x1, Pallas kernels, back(): pl.pallas_call(back_kernel, out_shape=[sd((4, 32, 2048), BF), sd((4, 32,...  90.3 us
    pallas_call x1, Pallas kernels, finish(): pl.pallas_call(finish_kernel, out_shape=[sd((2, 1, 64, 2048), BF), sd((2,...  6.52 us

profile of v1, /device:TPU:1, one launch (start us, length us, event | category | flops | bytes accessed | tf_op | source)
XLA Modules:
  0.0 196.2 jit_solution(5346770349655863939)
XLA Ops:
  0.6 98.6 %front.1 = (bf16[2048,1536]{1,0:T(8,128)(2,1)}, bf16[2048,512]{1,0:T(8,128)(2,1)}, f32[2,32,1024]{2,1,0:T(8,128)}, bf16[2,128,1024]{2,1,0:T(8,128)(2,1)}, f32[2,...) custom-call(bf16[2,64,2048]{2,1,0:T(8,128)(2,1)} %bitcast.9, ...), custom_call_target="tpu_custom_call" | custom-call | tf_op jit(solution)/shard_map/front/pallas_call | solution.py:758
  99.3 90.3 %back.1 = (bf16[4,32,2048]{2,1,0:T(8,128)(2,1)}, bf16[4,32,2048]{2,1,0:T(8,128)(2,1)}, bf16[4,4,4,2,32,512]{5,4,3,2,1,0:T(8,128)(2,1)}, f32[4,32,256]{2,1,0:T(8,...) custom-call(f32[32,2176]{1,0:T(8,128)} %get-tuple-element.31.dxe_in, bf16[2,64,2048]{2,1,0:T(8,128)(2,1)} %bitcast.10, ...), custom_call_target="tpu_custom_call" | custom-call | tf_op jit(solution)/shard_map/back/pallas_call | solution.py:1377
  189.5 6.5 %finish.1 = (bf16[2,1,64,2048]{3,2,1,0:T(8,128)(2,1)}, f32[2,1,64,2048]{3,2,1,0:T(8,128)}, f32[3,1024,512]{2,1,0:T(8,128)}, f32[1024,512]{1,0:T(8,128)}, f32[2,1...) custom-call(bf16[4,32,2048]{2,1,0:T(8,128)(2,1)} %get-tuple-element., ...), custom_call_target="tpu_custom_call" | custom-call | tf_op jit(solution)/shard_map/finish/pallas_call | solution.py:1353
